TPU v7x, 256 devices: a whole 4x4x8 slice. The times are simulated.
256 devices in a mesh: pts: 32 (over y, x, core), cam: 8 (over z).
Axes of the slice: x: 4, y: 4, z: 8, core: 2. Of those that a mesh axis runs over, the one named last changes fastest.
Arguments:
- jac_camera: bfloat16 [8, 18, 4, 4096], P('cam', None, None, 'pts'), may hold values from -4 to 4
- jac_point: bfloat16 [8, 6, 4, 4096], P('cam', None, None, 'pts'), may hold values from -6 to 6
- obs_camera: int32 [8, 4, 4096], P('cam', None, 'pts'), may hold values from 0 to 1023, as said below
- pair_groups: int32 [8, 2], P('cam'), may hold values from 0 to 7, as said below
- pair_points: int32 [8], P('cam'), may hold values from 512 to 4096, as said below
- damping: float32 [1], replicated, may hold values from 0.5 to 2
- rhs: float32 [8, 9, 128], replicated, may hold values from -6 to 6
Outputs:
- tiles: float32 [8, 2304, 2304], P('cam', 'pts')
- solution: float32 [8, 9, 128], replicated
Inputs may be any that keep to these rules, and one draw needn't show every extreme that they name: `pair_groups`: each pair names two different groups, and every group lies in exactly two pairs. `obs_camera`: the 4 cameras of a point are different and lie in the two groups of the point's pair. `pair_points`: slots at or beyond this count are padding; at least one pair is full in every draw.
All inputs are finite; a program needn't handle non-finite values.
Results may differ from a plain program's by a relative error of at most 0.0013.
Values may be sent and summed in bfloat16 or wider, within the bound.
A program may use at most 128 MiB of HBM per device.

v0:
```python
import functools
import jax
import jax.numpy as jnp
from jax import lax
from jax.experimental import pallas as pl
from jax.experimental.pallas import tpu as pltpu
from jax.sharding import PartitionSpec as P

F32 = jnp.float32
BF16 = jnp.bfloat16
ROWS = 112
XROWS = 104


def iota(shape, dim):
    return lax.broadcasted_iota(jnp.int32, shape, dim)


def sym(a, b):
    return (a, b) if a <= b else (b, a)


def point_blocks(x_ref, b_ref, b8_ref, dg_ref, slot_ref, damp, live, i_low, i_high):
    def load(q):
        return x_ref[pl.ds(q, 8, stride=XROWS), :]

    def rounded(value):
        return value.astype(BF16).astype(F32)

    for k in range(4):
        slot_ref[pl.ds(k * 8, 8), :] = jnp.where(live, load(96 + k), -1.0)
    jp = {(r, j, k): load(72 + (3 * r + j) * 4 + k) for r in range(2) for j in range(3) for k in range(4)}
    normal = {}
    for a in range(3):
        for b in range(a, 3):
            total = None
            for k in range(4):
                for r in range(2):
                    term = jp[r, a, k] * jp[r, b, k]
                    total = term if total is None else total + term
            normal[a, b] = total + damp if a == b else total
    n00, n01, n02 = normal[0, 0], normal[0, 1], normal[0, 2]
    n11, n12, n22 = normal[1, 1], normal[1, 2], normal[2, 2]
    c00 = n11 * n22 - n12 * n12
    c01 = n02 * n12 - n01 * n22
    c02 = n01 * n12 - n02 * n11
    c11 = n00 * n22 - n02 * n02
    c12 = n01 * n02 - n00 * n12
    c22 = n00 * n11 - n01 * n01
    scale = 1.0 / (n00 * c00 + n01 * c01 + n02 * c02)
    inv = {(0, 0): c00 * scale, (0, 1): c01 * scale, (0, 2): c02 * scale,
           (1, 1): c11 * scale, (1, 2): c12 * scale, (2, 2): c22 * scale}
    weighted = {}
    for k in range(4):
        for r in range(2):
            for l in range(3):
                weighted[r, k, l] = sum(jp[r, j, k] * inv[sym(j, l)] for j in range(1, 3)) + jp[r, 0, k] * inv[sym(0, l)]
    reduced = {}
    for a in range(8):
        for b in range(a, 8):
            k, r, m, s = a // 2, a % 2, b // 2, b % 2
            value = weighted[r, k, 0] * jp[s, 0, m] + weighted[r, k, 1] * jp[s, 1, m] + weighted[r, k, 2] * jp[s, 2, m]
            reduced[a, b] = 1.0 - value if a == b else -value

    def red(k, r, m, s):
        return reduced[sym(2 * k + r, 2 * m + s)]

    def camera(r, i, k):
        return load((9 * r + i) * 4 + k)

    for m in range(4):
        right = {(s, j): camera(s, j, m) for s in range(2) for j in range(9)}
        for j in range(9):
            parts = [
                rounded(right[0, j] * red(m, 0, m, s) + right[1, j] * red(m, 1, m, s)) * right[s, j]
                for s in range(2)
            ]
            dg_ref[pl.ds(m * 128 + j, 8, stride=16), :] = parts[0] + parts[1]
        for k in range(4):
            for which, i in enumerate((i_low, i_high)):
                left = [camera(r, i, k) for r in range(2)]
                mixed = [
                    rounded(left[0] * red(k, 0, m, s) + left[1] * red(k, 1, m, s)) for s in range(2)
                ]
                base = (which * 16 + k * 4 + m)
                for j in range(9):
                    value = mixed[0] * right[0, j] + mixed[1] * right[1, j]
                    if j < 8:
                        b_ref[pl.ds(base * 64 + j, 8, stride=8), :] = value
                    else:
                        b8_ref[pl.ds(base * 8, 8), :] = value


def twice(value):
    return jnp.concatenate([value, value], axis=0).astype(BF16)


def build_source(s, l_ref, r_ref, pb_ref, b_ref, b8_ref, dg_ref, slot_ref, target_ref, target8_ref, iota_ref, which_i):
    def row(ref, index):
        return jnp.broadcast_to(ref[pl.ds(index, 1), :], (8, 128))

    slots = [twice(row(slot_ref, k * 8 + s)) for k in range(4)]
    zero = jnp.zeros((16, 128), BF16)
    one = jnp.ones((16, 128), BF16)
    for b in range(16):
        value = iota_ref[pl.ds(b * 16, 16), :]
        for m in range(4):
            r_ref[pl.ds(b * 16, 16), pl.ds(m * 128, 128)] = jnp.where(slots[m] == value, one, zero)
    for which in range(2):
        for km in range(16):
            base = pl.multiple_of(((which * 16 + km) * 8 + s) * 8, 8)
            pb_ref[which, pl.ds(km * 16, 16), :] = twice(b_ref[pl.ds(base, 8), :])

    def choose(masks, values):
        value = zero
        for k in range(4):
            value = jnp.where(masks[k], values[k], value)
        return value

    for g in range(9):
        which = which_i[g]
        ops = [pb_ref[which, pl.ds(km * 16, 16), :] for km in range(16)]
        for b in range(4):
            first = (g * 4 + b) * 16
            target = target_ref[pl.ds(first, 16), :]
            masks = [slots[k] == target for k in range(4)]
            for m in range(4):
                l_ref[pl.ds(first, 16), pl.ds(m * 128, 128)] = choose(masks, [ops[k * 4 + m] for k in range(4)])
    for b in range(5):
        target = target8_ref[pl.ds(b * 16, 16), :]
        masks = [slots[k] == target for k in range(4)]
        low, high = which_i[2 * b], which_i[min(2 * b + 1, 8)]
        for m in range(4):
            values = []
            for k in range(4):
                km = k * 4 + m
                both = jnp.concatenate(
                    [row(b8_ref, (low * 16 + km) * 8 + s), row(b8_ref, (high * 16 + km) * 8 + s)], axis=0
                )
                values.append(both.astype(BF16))
            l_ref[pl.ds(576 + b * 16, 16), pl.ds(m * 128, 128)] = choose(masks, values)
    for m in range(4):
        base = pl.multiple_of((m * 8 + s) * 16, 16)
        l_ref[pl.ds(656, 16), pl.ds(m * 128, 128)] = dg_ref[pl.ds(base, 16), :].astype(BF16)


def place(position):
    first_row = position * 72
    half = position // 16
    inside = first_row - half * 1152
    i_low = inside // 128
    start = inside - i_low * 128
    i_high = jnp.minimum(i_low + 1, 8)
    which_i = [(start + 8 * g) // 128 for g in range(9)]
    return half, start, i_low, i_high, which_i


def prepare(position, target_ref, target8_ref, iota_ref, dg_ref):
    half, start, _, _, _ = place(position)

    def slot_of(r):
        return half * 128 + (start + r) % 128

    target_ref[...] = slot_of(iota((576, 128), 0) // 8).astype(F32).astype(BF16)
    row8 = iota((80, 128), 0)
    target8_ref[...] = jnp.where(row8 < 72, slot_of(row8), -2).astype(F32).astype(BF16)
    iota_ref[...] = iota((256, 128), 0).astype(F32).astype(BF16)
    dg_ref[...] = jnp.zeros_like(dg_ref)


def group_work(group, read_chunk, count, damp, position, out_acc, scr, first):
    (x_ref, b_ref, b8_ref, dg_ref, slot_ref, l_ref, r_ref, pb_ref, target_ref, target8_ref, iota_ref) = scr
    _, _, i_low, i_high, which_i = place(position)

    def widen(s, carry):
        x_ref[pl.ds(pl.multiple_of(s * XROWS, 8), XROWS), :] = read_chunk(group * 8 + s)[:XROWS].astype(F32)
        return carry

    lax.fori_loop(0, 8, widen, 0)
    index = (group * 8 + iota((8, 128), 0)) * 128 + iota((8, 128), 1)
    point_blocks(x_ref, b_ref, b8_ref, dg_ref, slot_ref, damp, index < count, i_low, i_high)

    def build(s, slot):
        build_source(s, l_ref.at[slot], r_ref.at[slot], pb_ref.at[slot], b_ref, b8_ref, dg_ref, slot_ref, target_ref, target8_ref, iota_ref, which_i)

    def product(slot):
        value = lax.dot_general(l_ref[slot], r_ref[slot], (((1,), (1,)), ((), ())), preferred_element_type=F32)
        out_acc[0] += value[:, :128]
        out_acc[1] += value[:, 128:]

    build(0, 0)

    def pair(t, carry):
        build(2 * t + 1, 1)
        product(0)
        build(jnp.minimum(2 * t + 2, 7), 0)
        product(1)
        return carry

    lax.fori_loop(0, 4, pair, 0)


def scratch():
    return [
        pltpu.VMEM((8 * XROWS, 128), F32),
        pltpu.VMEM((2 * 16 * 64, 128), F32),
        pltpu.VMEM((2 * 16 * 8, 128), F32),
        pltpu.VMEM((4 * 8 * 16, 128), F32),
        pltpu.VMEM((4 * 8, 128), F32),
        pltpu.VMEM((2, 672, 512), BF16),
        pltpu.VMEM((2, 256, 512), BF16),
        pltpu.VMEM((2, 2, 256, 128), BF16),
        pltpu.VMEM((576, 128), BF16),
        pltpu.VMEM((80, 128), BF16),
        pltpu.VMEM((256, 128), BF16),
    ]


def unpack_tile(acc_ref, tile_ref):
    for g in range(9):
        for h in range(2):
            for j in range(8):
                tile_ref[pl.ds(g * 8, 8), pl.ds(h * 1152 + j * 128, 128)] = acc_ref[h, pl.ds(g * 64 + j, 8, stride=8), :]
            tile_ref[pl.ds(g * 8, 8), pl.ds(h * 1152 + 1024, 128)] = acc_ref[h, pl.ds(576 + g * 8, 8), :]


def tile_kernel(count_ref, damp_ref, gather_ref, tile_ref, diag_ref, acc_ref, *scr):
    position = lax.axis_index("pts")
    prepare(position, scr[8], scr[9], scr[10], scr[3])
    acc_ref[...] = jnp.zeros_like(acc_ref)

    def loop(group, carry):
        group_work(group, lambda s: gather_ref[s], count_ref[0], damp_ref[0], position, acc_ref, scr, False)
        return carry

    lax.fori_loop(0, 4, loop, 0)
    unpack_tile(acc_ref, tile_ref)
    for h in range(2):
        diag_ref[h] = acc_ref[h, pl.ds(656, 16), :]


def tile_call(count, damp, gathered):
    vm = pl.BlockSpec(memory_space=pltpu.VMEM)
    sm = pl.BlockSpec(memory_space=pltpu.SMEM)
    return pl.pallas_call(
        tile_kernel,
        out_shape=(jax.ShapeDtypeStruct((72, 2304), F32), jax.ShapeDtypeStruct((2, 16, 128), F32)),
        in_specs=[sm, sm, vm],
        out_specs=(vm, vm),
        scratch_shapes=[pltpu.VMEM((2, 672, 128), F32)] + scratch(),
        compiler_params=pltpu.CompilerParams(vmem_limit_bytes=40 * 2**20),
        name="tile_rows",
    )(count, damp, gathered)


def body(jac_camera, jac_point, obs_camera, pair_groups, pair_points, damping, rhs):
    first, second = pair_groups[0, 0], pair_groups[0, 1]
    cameras = obs_camera[0]
    slot = jnp.where(cameras // 128 == second, 128, 0) + cameras % 128
    packed = jnp.concatenate(
        [jac_camera[0].reshape(72, 128), jac_point[0].reshape(24, 128), slot.astype(BF16), jnp.zeros((12, 128), BF16)], axis=0
    )
    gathered = lax.all_gather(packed, "pts", axis=0, tiled=False)
    tile, diag = tile_call(pair_points, damping, gathered)
    diag = diag[:, :9]
    d = damping[0]
    fh = (jnp.arange(8) == first).astype(F32)[:, None, None]
    sh = (jnp.arange(8) == second).astype(F32)[:, None, None]
    diagonal = lax.psum(fh * diag[0] + sh * diag[1], "cam") + d
    position = lax.axis_index("pts")

    def tvec(v):
        return jnp.concatenate([v[first].reshape(-1), v[second].reshape(-1)])

    z = rhs / diagonal
    p = z
    rz = jnp.sum(rhs * z)
    y = jnp.sum(tile * tvec(p)[None, :], axis=1)
    whole = lax.dynamic_update_slice_in_dim(jnp.zeros((2304,), F32), y, position * 72, 0).reshape(2, 9, 128)
    q = lax.psum(fh * whole[0] + sh * whole[1], ("pts", "cam")) + d * p
    alpha = rz / jnp.sum(p * q)
    x = alpha * p
    r = rhs - alpha * q
    z = r / diagonal
    new = jnp.sum(r * z)
    p = z + (new / rz) * p
    tv = tvec(p)
    y = jnp.sum(tile * tv[None, :], axis=1)
    own = lax.dynamic_slice_in_dim(tv, position * 72, 72, 0)
    pq = lax.psum(jnp.sum(own * y), ("pts", "cam")) + d * jnp.sum(p * p)
    x = x + (new / pq) * p
    return tile[None], x


def solution(mesh):
    placed = (P("cam", None, None, "pts"), P("cam", None, None, "pts"), P("cam", None, "pts"), P("cam", None), P("cam"), P(), P())
    return jax.shard_map(body, mesh=mesh, in_specs=placed, out_specs=(P("cam", "pts", None), P()), check_vma=False)
```

profile of v0, /device:TPU:1, one launch (start us, length us, event | category | flops | bytes accessed | tf_op | source)
XLA Modules:
  0.0 243.5 jit_solution(7199586979442554553)
XLA Ops:
  0.6 0.0 copy-start.3
  0.6 0.0 copy-start.2
  1.3 0.0 copy-done.3
  1.3 0.6 fusion.7
  1.9 1.3 fusion.3
  3.2 0.1 pad.7.clone
  3.3 0.0 copy-done.2
  3.3 0.8 maximum_maximum_fusion
  4.0 26.6 %all-gather = bf16[3584,128]{1,0:T(8,128)(2,1)S(1)} all-gather(bf16[112,128]{1,0:T(8,128)(2,1)S(1)} %maximum_maximum_fusion), channel_id=2, replica_groups=mesh['pts'=32,'cam'=8] {'pts'}, dimensions={0}, use_global_device_ids=true | all-gather | bytes 946176 | tf_op jit(solution)/shard_map/all_gather | solution.py:263
  31.3 17.8 %tile_rows.1 = (f32[72,2304]{1,0:T(8,128)}, f32[2,16,128]{2,1,0:T(8,128)S(1)}) custom-call(s32[1]{0:T(128)S(6)} %copy.34.count_ref, f32[1]{0:T(128)} %copy.35.damp_ref, bf16[32,112,128]{2,1,0:T(8,128)(2,1)S(1)} %bitcast.47), custom_call_target="tpu_custom_call" | custom-call | tf_op jit(solution)/shard_map/tile_rows/pallas_call | solution.py:245
  49.0 0.6 compare_convert_fusion
  49.6 0.7 compare_convert_fusion.1
  50.3 0.1 multiply_add_fusion.4
  50.4 0.0 copy-start.1
  50.4 26.5 %psum.21 = f32[8,9,128]{2,1,0:T(8,128)S(1)} all-reduce(f32[8,9,128]{2,1,0:T(8,128)S(1)} %multiply_add_fusion.4), channel_id=1, replica_groups=mesh['pts'=32,'cam'=8] {'cam'}, use_global_device_ids=true, to_apply=%region_0.1 | all-reduce | flops 9216 | bytes 73728 | tf_op jit(solution)/shard_map/psum | solution.py:269
  76.9 0.0 copy-done.1
  80.7 0.0 copy-start
  80.7 1.3 multiply_reduce_fusion.1
  82.0 0.3 dynamic_update_slice.3
  82.3 0.1 multiply_add_fusion.3
  82.4 79.8 %psum.22 = f32[8,9,128]{2,1,0:T(8,128)S(1)} all-reduce(f32[8,9,128]{2,1,0:T(8,128)S(1)} %multiply_add_fusion.3), channel_id=1, replica_groups=mesh['pts'=32,'cam'=8] {'pts','cam'}, use_global_device_ids=true, to_apply=%region_3.4 | all-reduce | flops 9216 | bytes 73728 | tf_op jit(solution)/shard_map/psum | solution.py:280
  162.2 0.7 multiply_reduce_fusion.4
  164.2 0.7 multiply_reduce_fusion.3
  166.2 0.6 multiply_reduce_fusion.2
  166.8 0.0 copy-done
  166.8 0.2 multiply_reduce_fusion
  167.0 0.7 multiply_reduce_fusion.5
  167.7 73.3 %psum.23 = f32[]{:T(128)} all-reduce(f32[]{:T(128)} %multiply_reduce_fusion.5), channel_id=1, replica_groups=mesh['pts'=32,'cam'=8] {'pts','cam'}, use_global_device_ids=true, to_apply=%region_8.9 | all-reduce | flops 1 | bytes 8 | tf_op jit(solution)/shard_map/psum | solution.py:290
  242.9 0.6 copy.12
  (10 shorter events, 0.1 us)
Async XLA Ops:
  0.6 0.7 copy-start.3
  0.6 2.6 %copy-start.2 = (bf16[1,18,4,128]{3,2,1,0:T(4,128)(2,1)S(1)}, bf16[1,18,4,128]{3,2,1,0:T(4,128)(2,1)}, u32[]{:S(2)}) copy-start(bf16[1,18,4,128]{3,2,1,0:T(4,128)(2,1)} %param.7) | copy-start | bytes 55300
  50.4 26.5 %copy-start.1 = (f32[8,9,128]{2,0,1:T(8,128)S(1)}, f32[8,9,128]{2,0,1:T(8,128)}, u32[]{:S(2)}) copy-start(f32[8,9,128]{2,0,1:T(8,128)} %param.13) | copy-start | bytes 110596
  80.7 86.1 %copy-start = (f32[72,2304]{1,0:T(8,128)S(1)}, f32[72,2304]{1,0:T(8,128)}, u32[]{:S(2)}) copy-start(f32[72,2304]{1,0:T(8,128)} %get-tuple-element.4) | copy-start | bytes 1990660
where the time goes:
time: 244 us
  blocking collectives  206 us (84%)
  Pallas kernels  17.8 us (7%)
  between operations  10.3 us (4%)
  other arithmetic  7.73 us (3%)
    psum x1, blocking collectives, body(): q = lax.psum(fh * whole[0] + sh * whole[1], ('pts', 'cam')) + d * p  79.8 us
    psum x1, blocking collectives, body(): pq = lax.psum(jnp.sum(own * y), ('pts', 'cam')) + d * jnp.sum(p * p)  73.3 us
    all_gather x1, blocking collectives, body(): gathered = lax.all_gather(packed, 'pts', axis=0, tiled=False)  26.6 us
    psum x1, blocking collectives, body(): diagonal = lax.psum(fh * diag[0] + sh * diag[1], 'cam') + d  26.5 us
    pallas_call x1, Pallas kernels, tile_call(): pl.pallas_call(tile_kernel, out_shape=(jax.ShapeDtypeStruct((72, 2304), F...  17.8 us

commit v1 on v0

--- a/solution.py
+++ b/solution.py
@@ -253,43 +253,257 @@
     )(count, damp, gathered)
 
 
+MESH = pl.DeviceIdType.MESH
+PTS = 32
+CAM = 8
+
+
+def here():
+    return lax.axis_index("pts"), lax.axis_index("cam")
+
+
+def plane_peer(d):
+    pts, cam = here()
+    return (pts + d) % PTS, cam
+
+
+def line_peer(d):
+    pts, cam = here()
+    return pts, (cam + d) % CAM
+
+
+def greet(plane, line):
+    barrier = pltpu.get_barrier_semaphore()
+    if plane:
+        def one(d, carry):
+            pl.semaphore_signal(barrier, inc=1, device_id=plane_peer(d), device_id_type=MESH)
+            return carry
+
+        lax.fori_loop(1, PTS, one, 0)
+    if line:
+        for d in range(1, CAM):
+            pl.semaphore_signal(barrier, inc=1, device_id=line_peer(d), device_id_type=MESH)
+
+
+def greeted(plane, line):
+    pl.semaphore_wait(pltpu.get_barrier_semaphore(), (PTS - 1 if plane else 0) + (CAM - 1 if line else 0))
+
+
+class Exchange:
+    def __init__(self, plane, block, send_sem, recv_sem):
+        self.size = PTS if plane else CAM
+        self.peer = plane_peer if plane else line_peer
+        self.me = here()[0 if plane else 1]
+        self.block, self.send_sem, self.recv_sem = block, send_sem, recv_sem
+
+    def copy(self, d):
+        return pltpu.make_async_remote_copy(
+            src_ref=self.block(self.me),
+            dst_ref=self.block(self.me),
+            send_sem=self.send_sem.at[d],
+            recv_sem=self.recv_sem.at[self.me],
+            device_id=self.peer(d),
+            device_id_type=MESH,
+        )
+
+    def arrival(self, d):
+        other = (self.me + d) % self.size
+        return pltpu.make_async_remote_copy(
+            src_ref=self.block(other),
+            dst_ref=self.block(other),
+            send_sem=self.send_sem.at[d],
+            recv_sem=self.recv_sem.at[other],
+            device_id=self.peer(d),
+            device_id_type=MESH,
+        )
+
+    def each(self, action):
+        def one(d, carry):
+            action(d)
+            return carry
+
+        lax.fori_loop(1, self.size, one, 0)
+
+    def send(self):
+        self.each(lambda d: self.copy(d).start())
+
+    def receive(self):
+        self.each(lambda d: self.arrival(d).wait_recv())
+
+    def sent(self):
+        self.each(lambda d: self.copy(d).wait_send())
+
+
+def pos_place(position):
+    first_row = position * 72
+    half = position // 16
+    inside = first_row % 1152
+    return half, inside // 128, inside % 128
+
+
+def spread(ref, index):
+    return jnp.broadcast_to(ref[pl.ds(index, 1), :], (8, 128))
+
+
+def total_of(values):
+    total = values[0]
+    for value in values[1:]:
+        total = total + value
+    return jnp.sum(jnp.sum(total, axis=0, keepdims=True), axis=1, keepdims=True)
+
+
+def solve(tile_ref, diag_block, groups_ref, damp, rhs_ref, out_ref, zd_ref, v_ref, zq_ref, pq_ref, zs_ref, ps_ref, sems):
+    position, cam = here()
+    half, start, i_low, i_high, which_i = place(position)
+    group_of = [groups_ref[0, 0], groups_ref[0, 1]]
+    sub = iota((8, 128), 0)
+    lane = iota((8, 128), 1)
+    subf = sub.astype(F32)
+    for h in range(2):
+        tagged = jnp.where(iota((16, 128), 0) == 9, group_of[h].astype(F32), diag_block(h))
+        zd_ref[pl.ds(pl.multiple_of((cam * 2 + h) * 16, 16), 16), :] = tagged
+    zd = Exchange(False, lambda t: zd_ref.at[pl.ds(pl.multiple_of(t * 32, 32), 32), :], sems[0], sems[1])
+    zd.send()
+    zd.receive()
+    member = {(t, h): spread(zd_ref, (t * 2 + h) * 16 + 9) == subf for t in range(CAM) for h in range(2)}
+    residual = [rhs_ref[i] for i in range(9)]
+    diagonal = []
+    for i in range(9):
+        total = jnp.full((8, 128), damp, F32)
+        for t in range(CAM):
+            for h in range(2):
+                total = total + jnp.where(member[t, h], spread(zd_ref, (t * 2 + h) * 16 + i), 0.0)
+        diagonal.append(total)
+    precond = [residual[i] / diagonal[i] for i in range(9)]
+    inner = total_of([residual[i] * precond[i] for i in range(9)])
+    own_member = [spread(zd_ref, (t * 2 + half) * 16 + 9) == subf for t in range(CAM)]
+
+    def image_row(vector):
+        for i in range(9):
+            v_ref[pl.ds(i * 8, 8), :] = vector[i]
+        ops = [[spread(v_ref, j * 8 + group_of[h]) for j in range(9)] for h in range(2)]
+        placed = jnp.zeros((8, 128), F32)
+        for g in range(9):
+            total = None
+            for h in range(2):
+                for j in range(9):
+                    term = tile_ref[pl.ds(g * 8, 8), pl.ds((h * 9 + j) * 128, 128)] * ops[h][j]
+                    total = term if total is None else total + term
+            value = jnp.sum(total, axis=1, keepdims=True)
+            placed = placed + jnp.where(lane == (start + 8 * g + sub) % 128, value, 0.0)
+        return jnp.sum(placed, axis=0, keepdims=True)
+
+    zq_ref[pl.ds(cam, 1), :] = image_row(precond)
+    zq = Exchange(False, lambda t: zq_ref.at[pl.ds(t, 1), :], sems[2], sems[3])
+    zq.send()
+    zq.receive()
+    total = jnp.zeros((8, 128), F32)
+    for t in range(CAM):
+        total = total + jnp.where(own_member[t], spread(zq_ref, t), 0.0)
+    pq_ref[pl.ds(pl.multiple_of(position * 8, 8), 8), :] = total
+    pq = Exchange(True, lambda p: pq_ref.at[pl.ds(pl.multiple_of(p * 8, 8), 8), :], sems[4], sems[5])
+    pq.send()
+    pq.receive()
+    image = [damp * precond[i] for i in range(9)]
+    for p in range(PTS):
+        _, low, first = pos_place(p)
+        value = pq_ref[pl.ds(p * 8, 8), :]
+        if first + 72 > 128:
+            image[low] = image[low] + jnp.where(lane >= first, value, 0.0)
+            image[low + 1] = image[low + 1] + jnp.where(lane >= first, 0.0, value)
+        else:
+            image[low] = image[low] + value
+    alpha = inner / total_of([precond[i] * image[i] for i in range(9)])
+    residual = [residual[i] - alpha * image[i] for i in range(9)]
+    scaled = [residual[i] / diagonal[i] for i in range(9)]
+    inner_next = total_of([residual[i] * scaled[i] for i in range(9)])
+    beta = inner_next / inner
+    direction = [scaled[i] + beta * precond[i] for i in range(9)]
+    row = image_row(direction)
+    own_group = jnp.where(half == 0, group_of[0], group_of[1])
+    lane_row = iota((1, 128), 1)
+    own = jnp.where(
+        lane_row >= start, v_ref[pl.ds(i_low * 8 + own_group, 1), :], v_ref[pl.ds(i_high * 8 + own_group, 1), :]
+    )
+    zs_ref[pl.ds(cam, 1), :] = row * own
+    zs = Exchange(False, lambda t: zs_ref.at[pl.ds(t, 1), :], sems[6], sems[7])
+    zs.send()
+    zs.receive()
+    ps_ref[pl.ds(position, 1), :] = jnp.sum(zs_ref[...], axis=0, keepdims=True)
+    ps = Exchange(True, lambda p: ps_ref.at[pl.ds(p, 1), :], sems[8], sems[9])
+    ps.send()
+    ps.receive()
+    curvature = damp * total_of([value * value for value in direction]) + total_of(
+        [ps_ref[pl.ds(8 * n, 8), :] for n in range(4)]
+    )
+    second = inner_next / curvature
+    for i in range(9):
+        out_ref[i] = alpha * precond[i] + second * direction[i]
+    for exchange in (zd, zq, pq, zs, ps):
+        exchange.sent()
+
+
+def solve_scratch():
+    return [
+        pltpu.VMEM((CAM * 32, 128), F32),
+        pltpu.VMEM((72, 128), F32),
+        pltpu.VMEM((CAM, 128), F32),
+        pltpu.VMEM((PTS * 8, 128), F32),
+        pltpu.VMEM((CAM, 128), F32),
+        pltpu.VMEM((PTS, 128), F32),
+    ]
+
+
+def solve_sems():
+    return [pltpu.SemaphoreType.DMA((n,)) for n in (CAM, CAM, CAM, CAM, PTS, PTS, CAM, CAM, PTS, PTS)]
+
+
+def gather_kernel(packed_ref, out_ref, send_sem, recv_sem):
+    position, _ = here()
+    greet(True, False)
+    out_ref[position] = packed_ref[...]
+    greeted(True, False)
+    chunks = Exchange(True, lambda p: out_ref.at[p], send_sem, recv_sem)
+    chunks.send()
+    chunks.receive()
+    chunks.sent()
+
+
+def solve_kernel(groups_ref, damp_ref, tile_ref, diag_ref, rhs_ref, out_ref, *scr):
+    greet(True, True)
+    greeted(True, True)
+    solve(tile_ref, lambda h: diag_ref[h], groups_ref, damp_ref[0], rhs_ref, out_ref, *scr[:6], scr[6:])
+
+
 def body(jac_camera, jac_point, obs_camera, pair_groups, pair_points, damping, rhs):
-    first, second = pair_groups[0, 0], pair_groups[0, 1]
+    second = pair_groups[0, 1]
     cameras = obs_camera[0]
     slot = jnp.where(cameras // 128 == second, 128, 0) + cameras % 128
     packed = jnp.concatenate(
         [jac_camera[0].reshape(72, 128), jac_point[0].reshape(24, 128), slot.astype(BF16), jnp.zeros((12, 128), BF16)], axis=0
     )
-    gathered = lax.all_gather(packed, "pts", axis=0, tiled=False)
+    vm = pl.BlockSpec(memory_space=pltpu.VMEM)
+    sm = pl.BlockSpec(memory_space=pltpu.SMEM)
+    gathered = pl.pallas_call(
+        gather_kernel,
+        out_shape=jax.ShapeDtypeStruct((PTS, ROWS, 128), BF16),
+        in_specs=[vm],
+        out_specs=vm,
+        scratch_shapes=[pltpu.SemaphoreType.DMA((PTS,)), pltpu.SemaphoreType.DMA((PTS,))],
+        compiler_params=pltpu.CompilerParams(collective_id=0, has_side_effects=True, vmem_limit_bytes=16 * 2**20),
+        name="gather_points",
+    )(packed)
     tile, diag = tile_call(pair_points, damping, gathered)
-    diag = diag[:, :9]
-    d = damping[0]
-    fh = (jnp.arange(8) == first).astype(F32)[:, None, None]
-    sh = (jnp.arange(8) == second).astype(F32)[:, None, None]
-    diagonal = lax.psum(fh * diag[0] + sh * diag[1], "cam") + d
-    position = lax.axis_index("pts")
-
-    def tvec(v):
-        return jnp.concatenate([v[first].reshape(-1), v[second].reshape(-1)])
-
-    z = rhs / diagonal
-    p = z
-    rz = jnp.sum(rhs * z)
-    y = jnp.sum(tile * tvec(p)[None, :], axis=1)
-    whole = lax.dynamic_update_slice_in_dim(jnp.zeros((2304,), F32), y, position * 72, 0).reshape(2, 9, 128)
-    q = lax.psum(fh * whole[0] + sh * whole[1], ("pts", "cam")) + d * p
-    alpha = rz / jnp.sum(p * q)
-    x = alpha * p
-    r = rhs - alpha * q
-    z = r / diagonal
-    new = jnp.sum(r * z)
-    p = z + (new / rz) * p
-    tv = tvec(p)
-    y = jnp.sum(tile * tv[None, :], axis=1)
-    own = lax.dynamic_slice_in_dim(tv, position * 72, 72, 0)
-    pq = lax.psum(jnp.sum(own * y), ("pts", "cam")) + d * jnp.sum(p * p)
-    x = x + (new / pq) * p
-    return tile[None], x
+    solved = pl.pallas_call(
+        solve_kernel,
+        out_shape=jax.ShapeDtypeStruct((9, 8, 128), F32),
+        in_specs=[sm, sm, vm, vm, vm],
+        out_specs=vm,
+        scratch_shapes=solve_scratch() + solve_sems(),
+        compiler_params=pltpu.CompilerParams(collective_id=1, has_side_effects=True, vmem_limit_bytes=16 * 2**20),
+        name="solve_system",
+    )(pair_groups, damping, tile, diag, rhs.transpose(1, 0, 2))
+    return tile[None], solved.transpose(1, 0, 2)
 
 
 def solution(mesh):

time: 244 us -> 81.7 us (0.33)
  blocking collectives: 206 us -> 0 us
  Pallas kernels: 17.8 us -> 75.6 us
  between operations: 10.3 us -> 2.02 us
  other arithmetic: 7.73 us -> 1.43 us
    psum x3 -> x0, blocking collectives: 179 us -> none  [the longest x1 79.8 us: body(): q = lax.psum(fh * whole[0] + sh * whole[1], ('pts', 'cam')) + d * p]
    pallas_call x0 -> x2, Pallas kernels: none -> 57.9 us  [the longest x1 36.7 us: body(): pl.pallas_call(solve_kernel, out_shape=jax.ShapeDtypeStruct((9, 8, 128),...]
    all_gather x1 -> x0, blocking collectives: 26.6 us -> none  [body(): gathered = lax.all_gather(packed, 'pts', axis=0, tiled=False)]
    reduce_sum x6 -> x0, other arithmetic: 4.22 us -> none  [the longest x2 1.35 us: body(): pq = lax.psum(jnp.sum(own * y), ('pts', 'cam')) + d * jnp.sum(p * p)]
where the time goes in v1:
time: 81.7 us; the launch traced here: 81.5 us
  Pallas kernels  75.6 us (93%)
  local copies, waits for them, and re-layouts  2.39 us (3%)
  between operations  2.02 us (2%)
  other arithmetic  1.43 us (2%)
    pallas_call x1, Pallas kernels, body(): pl.pallas_call(solve_kernel, out_shape=jax.ShapeDtypeStruct((9, 8, 128),...  36.7 us
    pallas_call x1, Pallas kernels, body(): pl.pallas_call(gather_kernel, out_shape=jax.ShapeDtypeStruct((PTS, ROWS,...  21.2 us
    pallas_call x1, Pallas kernels, tile_call(): pl.pallas_call(tile_kernel, out_shape=(jax.ShapeDtypeStruct((72, 2304), F...  17.8 us
    unnamed x11, local copies, waits for them, and re-layouts  1.73 us

profile of v1, /device:TPU:1, one launch (start us, length us, event | category | flops | bytes accessed | tf_op | source)
XLA Modules:
  0.0 81.5 jit_solution(4361251631902067280)
XLA Ops:
  0.6 0.0 copy-start.4
  1.3 0.0 copy-start.2
  1.3 0.0 copy-start.3
  2.0 0.0 copy-done.2
  2.0 0.6 slice.3
  2.6 0.0 copy-done.4
  2.6 0.7 fusion.2
  3.2 0.1 pad.3.clone
  3.3 0.0 copy-done.3
  3.3 0.8 maximum_maximum_fusion.packed_ref
  4.1 21.2 %gather_points.1.gather_ref = bf16[32,112,128]{2,1,0:T(8,128)(2,1)S(1)} custom-call(bf16[112,128]{1,0:T(8,128)(2,1)S(1)} %maximum_maximum_fusion.packed_ref), custom_call_target="tpu_custom_call" | custom-call | tf_op jit(solution)/shard_map/gather_points/pallas_call | solution.py:487
  25.3 0.0 copy-start.1
  25.3 17.8 %tile_rows.1 = (f32[72,2304]{1,0:T(8,128)}, f32[2,16,128]{2,1,0:T(8,128)S(1)}) custom-call(s32[1]{0:T(128)S(6)} %copy.10.count_ref, f32[1]{0:T(128)S(6)} %copy.11.damp_ref, bf16[32,112,128]{2,1,0:T(8,128)(2,1)S(1)} %gather_points.1.gather_ref), custom_call_target="tpu_custom_call" | custom-call | tf_op jit(solution)/shard_map/tile_rows/pallas_call | solution.py:245
  43.0 0.0 copy-done.1
  43.0 0.0 copy-start
  43.0 1.1 %copy-done = f32[72,2304]{1,0:T(8,128)S(1)} copy-done((f32[72,2304]{1,0:T(8,128)S(1)}, f32[72,2304]{1,0:T(8,128)}, u32[]{:S(2)}) %copy-start) | copy-done | bytes 663576
  44.1 36.7 %solve_system.1 = f32[9,8,128]{2,1,0:T(8,128)S(1)} custom-call(s32[1,2]{1,0:T(1,128)S(1)} %copy-done.2, f32[1]{0:T(128)S(6)} %copy.11.damp_ref, f32[72,2304]{1,0:T(8,128)S(1)} %copy-done, f32[2,16,128]{2,1,0:T(8,128)S(1)} %get-tuple-element.5.diag_ref, f32[9,8,128]{2,1,0:T(8,128)S(1)} %bitcast.26), custom_call_target="tpu_custom_call" | custom-call | tf_op jit(solution)/shard_map/solve_system/pallas_call | solution.py:497
  80.9 0.6 copy.12
  (1 shorter events, 0.0 us)
Async XLA Ops:
  0.6 1.9 %copy-start.4 = (s32[1,4,128]{2,1,0:T(4,128)S(1)}, s32[1,4,128]{2,1,0:T(4,128)}, u32[]{:S(2)}) copy-start(s32[1,4,128]{2,1,0:T(4,128)} %param.9) | copy-start | bytes 6148
  1.3 0.7 copy-start.2
  1.3 2.0 %copy-start.3 = (bf16[1,18,4,128]{3,2,1,0:T(4,128)(2,1)S(1)}, bf16[1,18,4,128]{3,2,1,0:T(4,128)(2,1)}, u32[]{:S(2)}) copy-start(bf16[1,18,4,128]{3,2,1,0:T(4,128)(2,1)} %param.7) | copy-start | bytes 55300
  25.3 17.8 %copy-start.1 = (f32[8,9,128]{2,0,1:T(8,128)S(1)}, f32[8,9,128]{2,0,1:T(8,128)}, u32[]{:S(2)}) copy-start(f32[8,9,128]{2,0,1:T(8,128)} %param.13) | copy-start | bytes 110596
  43.0 1.1 %copy-start = (f32[72,2304]{1,0:T(8,128)S(1)}, f32[72,2304]{1,0:T(8,128)}, u32[]{:S(2)}) copy-start(f32[72,2304]{1,0:T(8,128)} %get-tuple-element.4.tile_ref) | copy-start | bytes 1990660

commit v2 on v1

--- a/solution.py
+++ b/solution.py
@@ -10,6 +10,7 @@
 BF16 = jnp.bfloat16
 ROWS = 112
 XROWS = 104
+UNROLL = 4
 
 
 def iota(shape, dim):
@@ -95,17 +96,27 @@
     return jnp.concatenate([value, value], axis=0).astype(BF16)
 
 
-def build_source(s, l_ref, r_ref, pb_ref, b_ref, b8_ref, dg_ref, slot_ref, target_ref, target8_ref, iota_ref, which_i):
-    def row(ref, index):
-        return jnp.broadcast_to(ref[pl.ds(index, 1), :], (8, 128))
-
-    slots = [twice(row(slot_ref, k * 8 + s)) for k in range(4)]
+def spread_row(ref, index):
+    return jnp.broadcast_to(ref[pl.ds(index, 1), :], (8, 128))
+
+
+def push_places(s, register, slot_ref, iota_ref):
+    slots = [twice(spread_row(slot_ref, k * 8 + s)) for k in range(4)]
     zero = jnp.zeros((16, 128), BF16)
     one = jnp.ones((16, 128), BF16)
-    for b in range(16):
-        value = iota_ref[pl.ds(b * 16, 16), :]
-        for m in range(4):
-            r_ref[pl.ds(b * 16, 16), pl.ds(m * 128, 128)] = jnp.where(slots[m] == value, one, zero)
+    places = [iota_ref[pl.ds(b * 16, 16), :] for b in range(16)]
+    for unit in range(2):
+        columns = [
+            jnp.concatenate([jnp.where(slots[m] == value, one, zero) for value in places], axis=0)
+            for m in (2 * unit, 2 * unit + 1)
+        ]
+        pltpu.matmul_push_rhs(jnp.concatenate(columns, axis=1), register, unit, transpose=True)
+    return slots
+
+
+def build_source(s, register, slots, accs, pb_ref, b_ref, b8_ref, dg_ref, target_ref, target8_ref, which_i):
+    row = spread_row
+    zero = jnp.zeros((16, 128), BF16)
     for which in range(2):
         for km in range(16):
             base = pl.multiple_of(((which * 16 + km) * 8 + s) * 8, 8)
@@ -117,19 +128,28 @@
             value = jnp.where(masks[k], values[k], value)
         return value
 
+    def feed(block, parts):
+        for unit in range(2):
+            left = jnp.concatenate([parts[2 * unit], parts[2 * unit + 1]], axis=1)
+            pltpu.matmul_acc_lhs(accs[unit][block], left, load_staged_rhs=register if block == 41 else None)
+
+    parts = []
+    for m in range(4):
+        base = pl.multiple_of((m * 8 + s) * 16, 16)
+        parts.append(dg_ref[pl.ds(base, 16), :].astype(BF16))
+    feed(41, parts)
     for g in range(9):
         which = which_i[g]
         ops = [pb_ref[which, pl.ds(km * 16, 16), :] for km in range(16)]
         for b in range(4):
-            first = (g * 4 + b) * 16
-            target = target_ref[pl.ds(first, 16), :]
+            target = target_ref[pl.ds((g * 4 + b) * 16, 16), :]
             masks = [slots[k] == target for k in range(4)]
-            for m in range(4):
-                l_ref[pl.ds(first, 16), pl.ds(m * 128, 128)] = choose(masks, [ops[k * 4 + m] for k in range(4)])
+            feed(g * 4 + b, [choose(masks, [ops[k * 4 + m] for k in range(4)]) for m in range(4)])
     for b in range(5):
         target = target8_ref[pl.ds(b * 16, 16), :]
         masks = [slots[k] == target for k in range(4)]
         low, high = which_i[2 * b], which_i[min(2 * b + 1, 8)]
+        parts = []
         for m in range(4):
             values = []
             for k in range(4):
@@ -138,10 +158,8 @@
                     [row(b8_ref, (low * 16 + km) * 8 + s), row(b8_ref, (high * 16 + km) * 8 + s)], axis=0
                 )
                 values.append(both.astype(BF16))
-            l_ref[pl.ds(576 + b * 16, 16), pl.ds(m * 128, 128)] = choose(masks, values)
-    for m in range(4):
-        base = pl.multiple_of((m * 8 + s) * 16, 16)
-        l_ref[pl.ds(656, 16), pl.ds(m * 128, 128)] = dg_ref[pl.ds(base, 16), :].astype(BF16)
+            parts.append(choose(masks, values))
+        feed(36 + b, parts)
 
 
 def place(position):
@@ -155,7 +173,8 @@
     return half, start, i_low, i_high, which_i
 
 
-def prepare(position, target_ref, target8_ref, iota_ref, dg_ref):
+def prepare(position, scr):
+    dg_ref, target_ref, target8_ref, iota_ref = scr[3], scr[6], scr[7], scr[8]
     half, start, _, _, _ = place(position)
 
     def slot_of(r):
@@ -168,36 +187,46 @@
     dg_ref[...] = jnp.zeros_like(dg_ref)
 
 
-def group_work(group, read_chunk, count, damp, position, out_acc, scr, first):
-    (x_ref, b_ref, b8_ref, dg_ref, slot_ref, l_ref, r_ref, pb_ref, target_ref, target8_ref, iota_ref) = scr
+def make_group(read_chunk, count, damp, position, dq_ref, scr, accs):
+    (x_ref, b_ref, b8_ref, dg_ref, slot_ref, pb_ref, target_ref, target8_ref, iota_ref) = scr
+    accs = (accs[:42], accs[42:])
     _, _, i_low, i_high, which_i = place(position)
 
-    def widen(s, carry):
-        x_ref[pl.ds(pl.multiple_of(s * XROWS, 8), XROWS), :] = read_chunk(group * 8 + s)[:XROWS].astype(F32)
-        return carry
-
-    lax.fori_loop(0, 8, widen, 0)
-    index = (group * 8 + iota((8, 128), 0)) * 128 + iota((8, 128), 1)
-    point_blocks(x_ref, b_ref, b8_ref, dg_ref, slot_ref, damp, index < count, i_low, i_high)
-
-    def build(s, slot):
-        build_source(s, l_ref.at[slot], r_ref.at[slot], pb_ref.at[slot], b_ref, b8_ref, dg_ref, slot_ref, target_ref, target8_ref, iota_ref, which_i)
-
-    def product(slot):
-        value = lax.dot_general(l_ref[slot], r_ref[slot], (((1,), (1,)), ((), ())), preferred_element_type=F32)
-        out_acc[0] += value[:, :128]
-        out_acc[1] += value[:, 128:]
-
-    build(0, 0)
-
-    def pair(t, carry):
-        build(2 * t + 1, 1)
-        product(0)
-        build(jnp.minimum(2 * t + 2, 7), 0)
-        product(1)
-        return carry
-
-    lax.fori_loop(0, 4, pair, 0)
+    def group(row):
+        def widen(s, carry):
+            x_ref[pl.ds(pl.multiple_of(s * XROWS, 8), XROWS), :] = read_chunk(row * 8 + s)[:XROWS].astype(F32)
+            return carry
+
+        lax.fori_loop(0, 8, widen, 0)
+        sub = iota((8, 128), 0)
+        index = ((row * 4 + sub % 4) * 2 + sub // 4) * 128 + iota((8, 128), 1)
+        point_blocks(x_ref, b_ref, b8_ref, dg_ref, slot_ref, damp, index < count, i_low, i_high)
+
+        def sources(t, carry):
+            first = t * UNROLL
+            slots = {}
+            for u in range(min(2, UNROLL)):
+                slots[u] = push_places(first + u, u % 2, slot_ref, iota_ref)
+            for u in range(UNROLL):
+                build_source(
+                    first + u, u % 2, slots[u], accs, pb_ref.at[u], b_ref, b8_ref, dg_ref, target_ref, target8_ref, which_i
+                )
+                if u + 2 < UNROLL:
+                    slots[u + 2] = push_places(first + u + 2, u % 2, slot_ref, iota_ref)
+            return carry
+
+        lax.fori_loop(0, 8 // UNROLL, sources, 0)
+        value = pltpu.matmul_pop(accs[0][41]) + pltpu.matmul_pop(accs[1][41])
+        for h in range(2):
+            dq_ref[row, h] = value[:, h * 128 : h * 128 + 128]
+
+    def finish(acc_ref):
+        for block in range(41):
+            value = pltpu.matmul_pop(accs[0][block]) + pltpu.matmul_pop(accs[1][block])
+            for h in range(2):
+                acc_ref[h, pl.ds(block * 16, 16), :] = value[:, h * 128 : h * 128 + 128]
+
+    return group, finish
 
 
 def scratch():
@@ -207,13 +236,15 @@
         pltpu.VMEM((2 * 16 * 8, 128), F32),
         pltpu.VMEM((4 * 8 * 16, 128), F32),
         pltpu.VMEM((4 * 8, 128), F32),
-        pltpu.VMEM((2, 672, 512), BF16),
-        pltpu.VMEM((2, 256, 512), BF16),
-        pltpu.VMEM((2, 2, 256, 128), BF16),
+        pltpu.VMEM((UNROLL, 2, 256, 128), BF16),
         pltpu.VMEM((576, 128), BF16),
         pltpu.VMEM((80, 128), BF16),
         pltpu.VMEM((256, 128), BF16),
     ]
+
+
+def accumulators():
+    return [pltpu.ACC(unit)((16, 256), F32) for unit in range(2) for _ in range(42)]
 
 
 def unpack_tile(acc_ref, tile_ref):
@@ -224,33 +255,11 @@
             tile_ref[pl.ds(g * 8, 8), pl.ds(h * 1152 + 1024, 128)] = acc_ref[h, pl.ds(576 + g * 8, 8), :]
 
 
-def tile_kernel(count_ref, damp_ref, gather_ref, tile_ref, diag_ref, acc_ref, *scr):
-    position = lax.axis_index("pts")
-    prepare(position, scr[8], scr[9], scr[10], scr[3])
-    acc_ref[...] = jnp.zeros_like(acc_ref)
-
-    def loop(group, carry):
-        group_work(group, lambda s: gather_ref[s], count_ref[0], damp_ref[0], position, acc_ref, scr, False)
-        return carry
-
-    lax.fori_loop(0, 4, loop, 0)
-    unpack_tile(acc_ref, tile_ref)
-    for h in range(2):
-        diag_ref[h] = acc_ref[h, pl.ds(656, 16), :]
-
-
-def tile_call(count, damp, gathered):
-    vm = pl.BlockSpec(memory_space=pltpu.VMEM)
-    sm = pl.BlockSpec(memory_space=pltpu.SMEM)
-    return pl.pallas_call(
-        tile_kernel,
-        out_shape=(jax.ShapeDtypeStruct((72, 2304), F32), jax.ShapeDtypeStruct((2, 16, 128), F32)),
-        in_specs=[sm, sm, vm],
-        out_specs=(vm, vm),
-        scratch_shapes=[pltpu.VMEM((2, 672, 128), F32)] + scratch(),
-        compiler_params=pltpu.CompilerParams(vmem_limit_bytes=40 * 2**20),
-        name="tile_rows",
-    )(count, damp, gathered)
+def total_diag(dq_ref, h):
+    total = dq_ref[0, h]
+    for n in range(1, 4):
+        total = total + dq_ref[n, h]
+    return total
 
 
 MESH = pl.DeviceIdType.MESH
@@ -290,48 +299,42 @@
 
 
 class Exchange:
-    def __init__(self, plane, block, send_sem, recv_sem):
+    def __init__(self, plane, blocks, sem):
         self.size = PTS if plane else CAM
         self.peer = plane_peer if plane else line_peer
         self.me = here()[0 if plane else 1]
-        self.block, self.send_sem, self.recv_sem = block, send_sem, recv_sem
+        self.blocks, self.sem = blocks, sem
 
     def copy(self, d):
+        own = self.blocks(self.me, 1)
         return pltpu.make_async_remote_copy(
-            src_ref=self.block(self.me),
-            dst_ref=self.block(self.me),
-            send_sem=self.send_sem.at[d],
-            recv_sem=self.recv_sem.at[self.me],
-            device_id=self.peer(d),
-            device_id_type=MESH,
+            src_ref=own, dst_ref=own, send_sem=self.sem.at[0], recv_sem=self.sem.at[1],
+            device_id=self.peer(d), device_id_type=MESH,
         )
 
-    def arrival(self, d):
-        other = (self.me + d) % self.size
+    def all_others(self):
+        others = self.blocks(0, self.size - 1)
         return pltpu.make_async_remote_copy(
-            src_ref=self.block(other),
-            dst_ref=self.block(other),
-            send_sem=self.send_sem.at[d],
-            recv_sem=self.recv_sem.at[other],
-            device_id=self.peer(d),
-            device_id_type=MESH,
+            src_ref=others, dst_ref=others, send_sem=self.sem.at[0], recv_sem=self.sem.at[1],
+            device_id=self.peer(1), device_id_type=MESH,
         )
 
-    def each(self, action):
+    def send(self):
         def one(d, carry):
-            action(d)
+            self.copy(d).start()
             return carry
 
         lax.fori_loop(1, self.size, one, 0)
 
-    def send(self):
-        self.each(lambda d: self.copy(d).start())
-
     def receive(self):
-        self.each(lambda d: self.arrival(d).wait_recv())
+        self.all_others().wait_recv()
 
     def sent(self):
-        self.each(lambda d: self.copy(d).wait_send())
+        self.all_others().wait_send()
+
+
+def blocks_of(ref, rows):
+    return lambda first, count: ref.at[pl.ds(first * rows if isinstance(first, int) else pl.multiple_of(first * rows, rows), count * rows), :]
 
 
 def pos_place(position):
@@ -352,7 +355,7 @@
     return jnp.sum(jnp.sum(total, axis=0, keepdims=True), axis=1, keepdims=True)
 
 
-def solve(tile_ref, diag_block, groups_ref, damp, rhs_ref, out_ref, zd_ref, v_ref, zq_ref, pq_ref, zs_ref, ps_ref, sems):
+def solve(tile_ref, diag_block, groups_ref, damp, rhs_ref, out_ref, zd_ref, v_ref, zq_ref, pq_ref, zs_ref, ps_ref, sems, meanwhile, settle):
     position, cam = here()
     half, start, i_low, i_high, which_i = place(position)
     group_of = [groups_ref[0, 0], groups_ref[0, 1]]
@@ -362,8 +365,9 @@
     for h in range(2):
         tagged = jnp.where(iota((16, 128), 0) == 9, group_of[h].astype(F32), diag_block(h))
         zd_ref[pl.ds(pl.multiple_of((cam * 2 + h) * 16, 16), 16), :] = tagged
-    zd = Exchange(False, lambda t: zd_ref.at[pl.ds(pl.multiple_of(t * 32, 32), 32), :], sems[0], sems[1])
+    zd = Exchange(False, blocks_of(zd_ref, 32), sems[0])
     zd.send()
+    meanwhile()
     zd.receive()
     member = {(t, h): spread(zd_ref, (t * 2 + h) * 16 + 9) == subf for t in range(CAM) for h in range(2)}
     residual = [rhs_ref[i] for i in range(9)]
@@ -394,14 +398,14 @@
         return jnp.sum(placed, axis=0, keepdims=True)
 
     zq_ref[pl.ds(cam, 1), :] = image_row(precond)
-    zq = Exchange(False, lambda t: zq_ref.at[pl.ds(t, 1), :], sems[2], sems[3])
+    zq = Exchange(False, blocks_of(zq_ref, 1), sems[1])
     zq.send()
     zq.receive()
     total = jnp.zeros((8, 128), F32)
     for t in range(CAM):
         total = total + jnp.where(own_member[t], spread(zq_ref, t), 0.0)
     pq_ref[pl.ds(pl.multiple_of(position * 8, 8), 8), :] = total
-    pq = Exchange(True, lambda p: pq_ref.at[pl.ds(pl.multiple_of(p * 8, 8), 8), :], sems[4], sems[5])
+    pq = Exchange(True, blocks_of(pq_ref, 8), sems[2])
     pq.send()
     pq.receive()
     image = [damp * precond[i] for i in range(9)]
@@ -426,11 +430,14 @@
         lane_row >= start, v_ref[pl.ds(i_low * 8 + own_group, 1), :], v_ref[pl.ds(i_high * 8 + own_group, 1), :]
     )
     zs_ref[pl.ds(cam, 1), :] = row * own
-    zs = Exchange(False, lambda t: zs_ref.at[pl.ds(t, 1), :], sems[6], sems[7])
+    zs = Exchange(False, blocks_of(zs_ref, 1), sems[3])
     zs.send()
+    for exchange in (zd, zq, pq):
+        exchange.sent()
+    settle()
     zs.receive()
     ps_ref[pl.ds(position, 1), :] = jnp.sum(zs_ref[...], axis=0, keepdims=True)
-    ps = Exchange(True, lambda p: ps_ref.at[pl.ds(p, 1), :], sems[8], sems[9])
+    ps = Exchange(True, blocks_of(ps_ref, 1), sems[4])
     ps.send()
     ps.receive()
     curvature = damp * total_of([value * value for value in direction]) + total_of(
@@ -439,8 +446,8 @@
     second = inner_next / curvature
     for i in range(9):
         out_ref[i] = alpha * precond[i] + second * direction[i]
-    for exchange in (zd, zq, pq, zs, ps):
-        exchange.sent()
+    zs.sent()
+    ps.sent()
 
 
 def solve_scratch():
@@ -455,54 +462,144 @@
 
 
 def solve_sems():
-    return [pltpu.SemaphoreType.DMA((n,)) for n in (CAM, CAM, CAM, CAM, PTS, PTS, CAM, CAM, PTS, PTS)]
-
-
-def gather_kernel(packed_ref, out_ref, send_sem, recv_sem):
-    position, _ = here()
-    greet(True, False)
-    out_ref[position] = packed_ref[...]
-    greeted(True, False)
-    chunks = Exchange(True, lambda p: out_ref.at[p], send_sem, recv_sem)
-    chunks.send()
-    chunks.receive()
-    chunks.sent()
-
-
-def solve_kernel(groups_ref, damp_ref, tile_ref, diag_ref, rhs_ref, out_ref, *scr):
+    return [pltpu.SemaphoreType.DMA((2,)) for _ in range(5)]
+
+
+def plane_offsets():
+    return [(dy, dx) for dy in (0, 3, 2, 1) for dx in range(4) if (dy, dx) != (0, 0)]
+
+
+def whole_kernel(count_in, damp_in, groups_in, camera_in, point_in, obs_in, rhs_in, tile_out, out_ref, gbuf, tile_ref, acc_ref, dq_ref, *scr):
+    work, rest = scr[:9], scr[9:]
+    vectors, rest = rest[:6], rest[6:]
+    sems, rest = rest[:5], rest[5:]
+    send_sem, recv_sem, share_send, share_recv, load_sem = rest[:5]
+    count_ref, damp_ref, groups_ref, camera_ref, point_ref, obs_ref, rhs_ref = rest[5:]
+    position, cam = here()
+    y, x, c = position // 8, position // 2 % 4, position % 2
+    inputs = (count_in, damp_in, groups_in, camera_in, point_in, obs_in, rhs_in)
+    loads = [pltpu.make_async_copy(src, dst, load_sem.at[n]) for n, (src, dst) in enumerate(zip(inputs, rest[5:]))]
+    for load in loads:
+        load.start()
     greet(True, True)
+    for load in loads:
+        load.wait()
+    cameras = obs_ref[...]
+    slot = jnp.where(cameras // 128 == groups_ref[0, 1], 128, 0) + cameras % 128
+    chunk = jnp.concatenate(
+        [camera_ref[...].astype(F32), point_ref[...].astype(F32), slot.astype(F32), jnp.zeros((12, 128), F32)], axis=0
+    )
+    gbuf[(y * 2 + c) * 4 + x] = chunk.astype(BF16)
+    prepare(position, work)
     greeted(True, True)
-    solve(tile_ref, lambda h: diag_ref[h], groups_ref, damp_ref[0], rhs_ref, out_ref, *scr[:6], scr[6:])
+
+    def spread_copy(dy, dx):
+        own = gbuf.at[(y * 2 + c) * 4 + x]
+        other = ((y + dy) % 4 * 4 + (x + dx) % 4) * 2 + c
+        return pltpu.make_async_remote_copy(
+            src_ref=own, dst_ref=own, send_sem=send_sem.at[0], recv_sem=recv_sem.at[y],
+            device_id=(other, cam), device_id_type=MESH,
+        )
+
+    def chunks(first, count):
+        where = gbuf.at[pl.ds(first, count)]
+        return lambda send, recv: pltpu.make_async_remote_copy(
+            src_ref=where, dst_ref=where, send_sem=send, recv_sem=recv,
+            device_id=(position + 1 - 2 * c, cam), device_id_type=MESH,
+        )
+
+    def share(row, core):
+        return chunks((row * 2 + core) * 4, 4)(share_send.at[row], share_recv.at[row])
+
+    for dy, dx in plane_offsets():
+        spread_copy(dy, dx).start()
+
+    def hand_on(row, count):
+        chunks((row * 2 + c) * 4, count)(send_sem.at[0], recv_sem.at[row]).wait_recv()
+        share(row, c).start()
+
+    def assemble(*accs):
+        group, finish = make_group(lambda s: gbuf[s], count_ref[0, 0], damp_ref[0, 0], position, dq_ref, work, accs)
+        hand_on(y, 3)
+        hand_on((y + 1) % 4, 4)
+
+        def one(step, carry):
+            row = (y + step) % 4
+            share(row, 1 - c).wait_recv()
+            group(row)
+
+            @pl.when(step < 2)
+            def _():
+                hand_on((y + step + 2) % 4, 4)
+
+            return carry
+
+        lax.fori_loop(0, 4, one, 0)
+        finish(acc_ref)
+
+    pl.run_scoped(assemble, *accumulators())
+    store = pltpu.make_async_copy(tile_ref, tile_out, load_sem.at[7])
+
+    def unpack():
+        unpack_tile(acc_ref, tile_ref)
+        store.start()
+
+    def settle():
+        store.wait()
+        chunks(0, 15)(send_sem.at[0], recv_sem.at[0]).wait_send()
+        for row in range(4):
+            share(row, c).wait_send()
+
+    solve(
+        tile_ref, lambda h: total_diag(dq_ref, h), groups_ref, damp_ref[0, 0], rhs_ref, out_ref, *vectors, sems,
+        unpack, settle,
+    )
+
+
+def hand_over(tile_in, solved_in, tile_out, solved_out, tile_buf, solved_buf, sem):
+    pieces = [pl.ds(24 * n, 24) for n in range(3)]
+    stages = [(tile_in.at[p, :], tile_buf.at[p, :], tile_out.at[p, :]) for p in pieces] + [(solved_in, solved_buf, solved_out)]
+    loads = [pltpu.make_async_copy(src, buf, sem.at[0, n]) for n, (src, buf, _) in enumerate(stages)]
+    stores = [pltpu.make_async_copy(buf, dst, sem.at[1, n]) for n, (_, buf, dst) in enumerate(stages)]
+    for load in loads:
+        load.start()
+    for load, store in zip(loads, stores):
+        load.wait()
+        store.start()
+    for store in stores:
+        store.wait()
 
 
 def body(jac_camera, jac_point, obs_camera, pair_groups, pair_points, damping, rhs):
-    second = pair_groups[0, 1]
-    cameras = obs_camera[0]
-    slot = jnp.where(cameras // 128 == second, 128, 0) + cameras % 128
-    packed = jnp.concatenate(
-        [jac_camera[0].reshape(72, 128), jac_point[0].reshape(24, 128), slot.astype(BF16), jnp.zeros((12, 128), BF16)], axis=0
+    vm = pl.BlockSpec(memory_space=pltpu.VMEM)
+    far = pl.BlockSpec(memory_space=pltpu.HBM)
+    tile, solved = pl.pallas_call(
+        whole_kernel,
+        out_shape=(jax.ShapeDtypeStruct((72, 2304), F32), jax.ShapeDtypeStruct((9, 8, 128), F32)),
+        in_specs=[far] * 7,
+        out_specs=(far, vm),
+        scratch_shapes=[pltpu.VMEM((PTS, ROWS, 128), BF16), pltpu.VMEM((72, 2304), F32), pltpu.VMEM((2, 656, 128), F32), pltpu.VMEM((4, 2, 16, 128), F32)]
+        + scratch()
+        + solve_scratch()
+        + solve_sems()
+        + [pltpu.SemaphoreType.DMA((n,)) for n in (1, 4, 4, 4, 8)]
+        + [pltpu.SMEM((1, 1), jnp.int32), pltpu.SMEM((1, 1), F32), pltpu.SMEM((1, 2), jnp.int32)]
+        + [pltpu.VMEM((72, 128), BF16), pltpu.VMEM((24, 128), BF16), pltpu.VMEM((4, 128), jnp.int32), pltpu.VMEM((9, 8, 128), F32)],
+        compiler_params=pltpu.CompilerParams(collective_id=0, has_side_effects=True, vmem_limit_bytes=60 * 2**20),
+        name="reduced_system",
+    )(
+        pair_points.reshape(1, 1), damping.reshape(1, 1), pair_groups, jac_camera[0].reshape(72, 128), jac_point[0].reshape(24, 128), obs_camera[0],
+        rhs.transpose(1, 0, 2),
     )
-    vm = pl.BlockSpec(memory_space=pltpu.VMEM)
-    sm = pl.BlockSpec(memory_space=pltpu.SMEM)
-    gathered = pl.pallas_call(
-        gather_kernel,
-        out_shape=jax.ShapeDtypeStruct((PTS, ROWS, 128), BF16),
-        in_specs=[vm],
-        out_specs=vm,
-        scratch_shapes=[pltpu.SemaphoreType.DMA((PTS,)), pltpu.SemaphoreType.DMA((PTS,))],
-        compiler_params=pltpu.CompilerParams(collective_id=0, has_side_effects=True, vmem_limit_bytes=16 * 2**20),
-        name="gather_points",
-    )(packed)
-    tile, diag = tile_call(pair_points, damping, gathered)
-    solved = pl.pallas_call(
-        solve_kernel,
-        out_shape=jax.ShapeDtypeStruct((9, 8, 128), F32),
-        in_specs=[sm, sm, vm, vm, vm],
-        out_specs=vm,
-        scratch_shapes=solve_scratch() + solve_sems(),
-        compiler_params=pltpu.CompilerParams(collective_id=1, has_side_effects=True, vmem_limit_bytes=16 * 2**20),
-        name="solve_system",
-    )(pair_groups, damping, tile, diag, rhs.transpose(1, 0, 2))
+    tile, solved = pl.pallas_call(
+        hand_over,
+        out_shape=(jax.ShapeDtypeStruct((72, 2304), F32), jax.ShapeDtypeStruct((9, 8, 128), F32)),
+        in_specs=[far] * 2,
+        out_specs=(far, far),
+        scratch_shapes=[pltpu.VMEM((72, 2304), F32), pltpu.VMEM((9, 8, 128), F32), pltpu.SemaphoreType.DMA((2, 4))],
+        compiler_params=pltpu.CompilerParams(vmem_limit_bytes=60 * 2**20),
+        name="hand_over",
+    )(tile, solved)
     return tile[None], solved.transpose(1, 0, 2)
 
 

time: 81.7 us -> 56.3 us (0.69)
  Pallas kernels: 75.6 us -> 54.2 us
  local copies, waits for them, and re-layouts: 2.39 us -> 0 us
  other arithmetic: 1.43 us -> 0 us
    pallas_call x3 -> x2, Pallas kernels: 75.6 us -> 54.2 us  [the longest x1 52.3 us: body(): pl.pallas_call(whole_kernel, out_shape=(jax.ShapeDtypeStruct((72, 2304),...]
    unnamed x11 -> x0, local copies, waits for them, and re-layouts: 1.73 us -> none
where the time goes in v2:
time: 56.3 us; the launch traced here: 56.1 us
  Pallas kernels  54.2 us (96%)
  between operations  1.93 us (3%)
    pallas_call x1, Pallas kernels, body(): pl.pallas_call(whole_kernel, out_shape=(jax.ShapeDtypeStruct((72, 2304),...  52.3 us
    pallas_call x1, Pallas kernels, body(): pl.pallas_call(hand_over, out_shape=(jax.ShapeDtypeStruct((72, 2304), F32...  1.91 us

profile of v2, /device:TPU:1, one launch (start us, length us, event | category | flops | bytes accessed | tf_op | source)
XLA Modules:
  0.0 56.1 jit_solution(4184255326017050978)
XLA Ops:
  1.9 52.3 %reduced_system.1 = (f32[72,2304]{1,0:T(8,128)}, f32[9,8,128]{2,1,0:T(8,128)}) custom-call(s32[1,1]{1,0:T(1,128)} %bitcast.8.count_in, f32[1,1]{1,0:T(1,128)} %bitcast.9.damp_in, s32[1,2]{1,0:T(1,128)} %groups_in.1, bf16[72,128]{1,0:T(8,128)(2,1)} %bitcast.11, bf16[24,128]{1,0:T(8,128)(2,1)} %bitcast.12, s32[4,128]{1,0:T(4,128)} %bitcast.13, ...), custom_call_target="tpu_custom_call" | custom-call | tf_op jit(solution)/shard_map/reduced_system/pallas_call | solution.py:576
  54.2 1.9 %hand_over.1 = (f32[72,2304]{1,0:T(8,128)}, f32[9,8,128]{2,1,0:T(8,128)}) custom-call(f32[72,2304]{1,0:T(8,128)} %get-tuple-element.6.tile_in, f32[9,8,128]{2,1,0:T(8,128)} %get-tuple-element.7.solved_in), custom_call_target="tpu_custom_call" | custom-call | tf_op jit(solution)/shard_map/hand_over/pallas_call | solution.py:594

commit v3 on v2

--- a/solution.py
+++ b/solution.py
@@ -21,15 +21,11 @@
     return (a, b) if a <= b else (b, a)
 
 
-def point_blocks(x_ref, b_ref, b8_ref, dg_ref, slot_ref, damp, live, i_low, i_high):
-    def load(q):
-        return x_ref[pl.ds(q, 8, stride=XROWS), :]
-
-    def rounded(value):
-        return value.astype(BF16).astype(F32)
-
-    for k in range(4):
-        slot_ref[pl.ds(k * 8, 8), :] = jnp.where(live, load(96 + k), -1.0)
+def rounded(value):
+    return value.astype(BF16).astype(F32)
+
+
+def geometry(load, damp):
     jp = {(r, j, k): load(72 + (3 * r + j) * 4 + k) for r in range(2) for j in range(3) for k in range(4)}
     normal = {}
     for a in range(3):
@@ -66,17 +62,34 @@
     def red(k, r, m, s):
         return reduced[sym(2 * k + r, 2 * m + s)]
 
+    return red
+
+
+def own_diagonal(x_ref, dg_ref, damp):
+    def load(q):
+        return x_ref[pl.ds(q, 1), :]
+
+    red = geometry(load, damp)
+    for m in range(4):
+        for j in range(9):
+            jac = [load((9 * r + j) * 4 + m) for r in range(2)]
+            parts = [rounded(jac[0] * red(m, 0, m, s) + jac[1] * red(m, 1, m, s)) * jac[s] for s in range(2)]
+            dg_ref[pl.ds(m * 16 + j, 1), :] = parts[0] + parts[1]
+
+
+def point_blocks(x_ref, b_ref, b8_ref, slot_ref, damp, live, i_low, i_high):
+    def load(q):
+        return x_ref[pl.ds(q, 8, stride=XROWS), :]
+
+    for k in range(4):
+        slot_ref[pl.ds(k * 8, 8), :] = jnp.where(live, load(96 + k), -1.0)
+    red = geometry(load, damp)
+
     def camera(r, i, k):
         return load((9 * r + i) * 4 + k)
 
     for m in range(4):
         right = {(s, j): camera(s, j, m) for s in range(2) for j in range(9)}
-        for j in range(9):
-            parts = [
-                rounded(right[0, j] * red(m, 0, m, s) + right[1, j] * red(m, 1, m, s)) * right[s, j]
-                for s in range(2)
-            ]
-            dg_ref[pl.ds(m * 128 + j, 8, stride=16), :] = parts[0] + parts[1]
         for k in range(4):
             for which, i in enumerate((i_low, i_high)):
                 left = [camera(r, i, k) for r in range(2)]
@@ -114,7 +127,7 @@
     return slots
 
 
-def build_source(s, register, slots, accs, pb_ref, b_ref, b8_ref, dg_ref, target_ref, target8_ref, which_i):
+def build_source(s, register, slots, accs, pb_ref, b_ref, b8_ref, target_ref, target8_ref, which_i):
     row = spread_row
     zero = jnp.zeros((16, 128), BF16)
     for which in range(2):
@@ -131,13 +144,8 @@
     def feed(block, parts):
         for unit in range(2):
             left = jnp.concatenate([parts[2 * unit], parts[2 * unit + 1]], axis=1)
-            pltpu.matmul_acc_lhs(accs[unit][block], left, load_staged_rhs=register if block == 41 else None)
-
-    parts = []
-    for m in range(4):
-        base = pl.multiple_of((m * 8 + s) * 16, 16)
-        parts.append(dg_ref[pl.ds(base, 16), :].astype(BF16))
-    feed(41, parts)
+            pltpu.matmul_acc_lhs(accs[unit][block], left, load_staged_rhs=register if block == 0 else None)
+
     for g in range(9):
         which = which_i[g]
         ops = [pb_ref[which, pl.ds(km * 16, 16), :] for km in range(16)]
@@ -187,9 +195,9 @@
     dg_ref[...] = jnp.zeros_like(dg_ref)
 
 
-def make_group(read_chunk, count, damp, position, dq_ref, scr, accs):
-    (x_ref, b_ref, b8_ref, dg_ref, slot_ref, pb_ref, target_ref, target8_ref, iota_ref) = scr
-    accs = (accs[:42], accs[42:])
+def make_group(read_chunk, count, damp, position, scr, accs):
+    (x_ref, b_ref, b8_ref, _, slot_ref, pb_ref, target_ref, target8_ref, iota_ref) = scr
+    accs = (accs[:41], accs[41:])
     _, _, i_low, i_high, which_i = place(position)
 
     def group(row):
@@ -200,7 +208,7 @@
         lax.fori_loop(0, 8, widen, 0)
         sub = iota((8, 128), 0)
         index = ((row * 4 + sub % 4) * 2 + sub // 4) * 128 + iota((8, 128), 1)
-        point_blocks(x_ref, b_ref, b8_ref, dg_ref, slot_ref, damp, index < count, i_low, i_high)
+        point_blocks(x_ref, b_ref, b8_ref, slot_ref, damp, index < count, i_low, i_high)
 
         def sources(t, carry):
             first = t * UNROLL
@@ -209,16 +217,13 @@
                 slots[u] = push_places(first + u, u % 2, slot_ref, iota_ref)
             for u in range(UNROLL):
                 build_source(
-                    first + u, u % 2, slots[u], accs, pb_ref.at[u], b_ref, b8_ref, dg_ref, target_ref, target8_ref, which_i
+                    first + u, u % 2, slots[u], accs, pb_ref.at[u], b_ref, b8_ref, target_ref, target8_ref, which_i
                 )
                 if u + 2 < UNROLL:
                     slots[u + 2] = push_places(first + u + 2, u % 2, slot_ref, iota_ref)
             return carry
 
         lax.fori_loop(0, 8 // UNROLL, sources, 0)
-        value = pltpu.matmul_pop(accs[0][41]) + pltpu.matmul_pop(accs[1][41])
-        for h in range(2):
-            dq_ref[row, h] = value[:, h * 128 : h * 128 + 128]
 
     def finish(acc_ref):
         for block in range(41):
@@ -234,7 +239,7 @@
         pltpu.VMEM((8 * XROWS, 128), F32),
         pltpu.VMEM((2 * 16 * 64, 128), F32),
         pltpu.VMEM((2 * 16 * 8, 128), F32),
-        pltpu.VMEM((4 * 8 * 16, 128), F32),
+        pltpu.VMEM((64, 128), F32),
         pltpu.VMEM((4 * 8, 128), F32),
         pltpu.VMEM((UNROLL, 2, 256, 128), BF16),
         pltpu.VMEM((576, 128), BF16),
@@ -244,7 +249,7 @@
 
 
 def accumulators():
-    return [pltpu.ACC(unit)((16, 256), F32) for unit in range(2) for _ in range(42)]
+    return [pltpu.ACC(unit)((16, 256), F32) for unit in range(2) for _ in range(41)]
 
 
 def unpack_tile(acc_ref, tile_ref):
@@ -255,13 +260,6 @@
             tile_ref[pl.ds(g * 8, 8), pl.ds(h * 1152 + 1024, 128)] = acc_ref[h, pl.ds(576 + g * 8, 8), :]
 
 
-def total_diag(dq_ref, h):
-    total = dq_ref[0, h]
-    for n in range(1, 4):
-        total = total + dq_ref[n, h]
-    return total
-
-
 MESH = pl.DeviceIdType.MESH
 PTS = 32
 CAM = 8
@@ -355,33 +353,39 @@
     return jnp.sum(jnp.sum(total, axis=0, keepdims=True), axis=1, keepdims=True)
 
 
-def solve(tile_ref, diag_block, groups_ref, damp, rhs_ref, out_ref, zd_ref, v_ref, zq_ref, pq_ref, zs_ref, ps_ref, sems, meanwhile, settle):
+def by_group(zd_ref, half, value):
+    groups = iota((8, 128), 0).astype(F32)
+    total = jnp.zeros((8, 128), F32)
+    for t in range(CAM):
+        total = total + jnp.where(spread(zd_ref, t * 8 + 1 + half) == groups, value(t), 0.0)
+    return total
+
+
+def solve(tile_ref, groups_ref, damp, rhs_ref, out_ref, zd_ref, pd_ref, v_ref, zq_ref, pq_ref, zs_ref, ps_ref, pd, sems, meanwhile, settle):
     position, cam = here()
     half, start, i_low, i_high, which_i = place(position)
     group_of = [groups_ref[0, 0], groups_ref[0, 1]]
     sub = iota((8, 128), 0)
     lane = iota((8, 128), 1)
-    subf = sub.astype(F32)
-    for h in range(2):
-        tagged = jnp.where(iota((16, 128), 0) == 9, group_of[h].astype(F32), diag_block(h))
-        zd_ref[pl.ds(pl.multiple_of((cam * 2 + h) * 16, 16), 16), :] = tagged
-    zd = Exchange(False, blocks_of(zd_ref, 32), sems[0])
-    zd.send()
     meanwhile()
-    zd.receive()
-    member = {(t, h): spread(zd_ref, (t * 2 + h) * 16 + 9) == subf for t in range(CAM) for h in range(2)}
+    pd.receive()
+
+    def assemble(ref, base):
+        sums = list(base)
+        for p in range(PTS):
+            _, low, first = pos_place(p)
+            value = ref[pl.ds(p * 8, 8), :]
+            if first + 72 > 128:
+                sums[low] = sums[low] + jnp.where(lane >= first, value, 0.0)
+                sums[low + 1] = sums[low + 1] + jnp.where(lane >= first, 0.0, value)
+            else:
+                sums[low] = sums[low] + value
+        return sums
+
     residual = [rhs_ref[i] for i in range(9)]
-    diagonal = []
-    for i in range(9):
-        total = jnp.full((8, 128), damp, F32)
-        for t in range(CAM):
-            for h in range(2):
-                total = total + jnp.where(member[t, h], spread(zd_ref, (t * 2 + h) * 16 + i), 0.0)
-        diagonal.append(total)
+    diagonal = assemble(pd_ref, [jnp.full((8, 128), damp, F32)] * 9)
     precond = [residual[i] / diagonal[i] for i in range(9)]
     inner = total_of([residual[i] * precond[i] for i in range(9)])
-    own_member = [spread(zd_ref, (t * 2 + half) * 16 + 9) == subf for t in range(CAM)]
-
     def image_row(vector):
         for i in range(9):
             v_ref[pl.ds(i * 8, 8), :] = vector[i]
@@ -398,25 +402,15 @@
         return jnp.sum(placed, axis=0, keepdims=True)
 
     zq_ref[pl.ds(cam, 1), :] = image_row(precond)
-    zq = Exchange(False, blocks_of(zq_ref, 1), sems[1])
+    zq = Exchange(False, blocks_of(zq_ref, 1), sems[0])
     zq.send()
     zq.receive()
-    total = jnp.zeros((8, 128), F32)
-    for t in range(CAM):
-        total = total + jnp.where(own_member[t], spread(zq_ref, t), 0.0)
+    total = by_group(zd_ref, half, lambda t: spread(zq_ref, t))
     pq_ref[pl.ds(pl.multiple_of(position * 8, 8), 8), :] = total
-    pq = Exchange(True, blocks_of(pq_ref, 8), sems[2])
+    pq = Exchange(True, blocks_of(pq_ref, 8), sems[1])
     pq.send()
     pq.receive()
-    image = [damp * precond[i] for i in range(9)]
-    for p in range(PTS):
-        _, low, first = pos_place(p)
-        value = pq_ref[pl.ds(p * 8, 8), :]
-        if first + 72 > 128:
-            image[low] = image[low] + jnp.where(lane >= first, value, 0.0)
-            image[low + 1] = image[low + 1] + jnp.where(lane >= first, 0.0, value)
-        else:
-            image[low] = image[low] + value
+    image = assemble(pq_ref, [damp * precond[i] for i in range(9)])
     alpha = inner / total_of([precond[i] * image[i] for i in range(9)])
     residual = [residual[i] - alpha * image[i] for i in range(9)]
     scaled = [residual[i] / diagonal[i] for i in range(9)]
@@ -430,14 +424,14 @@
         lane_row >= start, v_ref[pl.ds(i_low * 8 + own_group, 1), :], v_ref[pl.ds(i_high * 8 + own_group, 1), :]
     )
     zs_ref[pl.ds(cam, 1), :] = row * own
-    zs = Exchange(False, blocks_of(zs_ref, 1), sems[3])
+    zs = Exchange(False, blocks_of(zs_ref, 1), sems[2])
     zs.send()
-    for exchange in (zd, zq, pq):
+    for exchange in (pd, zq, pq):
         exchange.sent()
     settle()
     zs.receive()
     ps_ref[pl.ds(position, 1), :] = jnp.sum(zs_ref[...], axis=0, keepdims=True)
-    ps = Exchange(True, blocks_of(ps_ref, 1), sems[4])
+    ps = Exchange(True, blocks_of(ps_ref, 1), sems[3])
     ps.send()
     ps.receive()
     curvature = damp * total_of([value * value for value in direction]) + total_of(
@@ -452,7 +446,8 @@
 
 def solve_scratch():
     return [
-        pltpu.VMEM((CAM * 32, 128), F32),
+        pltpu.VMEM((CAM * 8, 128), F32),
+        pltpu.VMEM((PTS * 8, 128), F32),
         pltpu.VMEM((72, 128), F32),
         pltpu.VMEM((CAM, 128), F32),
         pltpu.VMEM((PTS * 8, 128), F32),
@@ -462,23 +457,52 @@
 
 
 def solve_sems():
-    return [pltpu.SemaphoreType.DMA((2,)) for _ in range(5)]
+    return [pltpu.SemaphoreType.DMA((2,)) for _ in range(4)]
 
 
 def plane_offsets():
     return [(dy, dx) for dy in (0, 3, 2, 1) for dx in range(4) if (dy, dx) != (0, 0)]
 
 
-def whole_kernel(count_in, damp_in, groups_in, camera_in, point_in, obs_in, rhs_in, tile_out, out_ref, gbuf, tile_ref, acc_ref, dq_ref, *scr):
+def partial_diagonal(x_ref, dg_ref, position, count, damp, part_ref, rows_out):
+    own_diagonal(x_ref, dg_ref, damp)
+    lane = iota((1, 128), 1)
+    live = position * 128 + lane < count
+    places = iota((256, 128), 0).astype(F32)
+    left, right = [], []
+    for k in range(4):
+        slot = jnp.where(live, x_ref[pl.ds(96 + k, 1), :], -1.0)
+        left.append(dg_ref[pl.ds(k * 16, 16), :].astype(BF16))
+        right.append((jnp.broadcast_to(slot, (256, 128)) == places).astype(F32).astype(BF16))
+
+    def product(*accs):
+        for unit in range(2):
+            pair = (2 * unit, 2 * unit + 1)
+            pltpu.matmul_push_rhs(jnp.concatenate([right[k] for k in pair], axis=1), 0, unit, transpose=True)
+            pltpu.matmul_acc_lhs(accs[unit], jnp.concatenate([left[k] for k in pair], axis=1), load_staged_rhs=0)
+        value = pltpu.matmul_pop(accs[0]) + pltpu.matmul_pop(accs[1])
+        for h in range(2):
+            part_ref[h] = value[:, h * 128 : h * 128 + 128]
+
+    pl.run_scoped(product, *[pltpu.ACC(unit)((16, 256), F32) for unit in range(2)])
+    for p in range(PTS):
+        h, low, first = pos_place(p)
+        row = part_ref[h, low : low + 1, :]
+        if first + 72 > 128:
+            row = jnp.where(lane >= first, row, part_ref[h, low + 1 : low + 2, :])
+        rows_out[p : p + 1, :] = row
+
+
+def whole_kernel(count_in, damp_in, groups_in, camera_in, point_in, obs_in, rhs_in, tile_out, out_ref, gbuf, tile_ref, acc_ref, part_ref, rows_out, rows_in, *scr):
     work, rest = scr[:9], scr[9:]
-    vectors, rest = rest[:6], rest[6:]
-    sems, rest = rest[:5], rest[5:]
-    send_sem, recv_sem, share_send, share_recv, load_sem = rest[:5]
-    count_ref, damp_ref, groups_ref, camera_ref, point_ref, obs_ref, rhs_ref = rest[5:]
+    vectors, rest = rest[:7], rest[7:]
+    sems, rest = rest[:4], rest[4:]
+    send_sem, recv_sem, share_send, share_recv, load_sem, row_sem, zd_sem, pd_sem = rest[:8]
+    count_ref, damp_ref, groups_ref, camera_ref, point_ref, obs_ref, rhs_ref = rest[8:]
     position, cam = here()
     y, x, c = position // 8, position // 2 % 4, position % 2
     inputs = (count_in, damp_in, groups_in, camera_in, point_in, obs_in, rhs_in)
-    loads = [pltpu.make_async_copy(src, dst, load_sem.at[n]) for n, (src, dst) in enumerate(zip(inputs, rest[5:]))]
+    loads = [pltpu.make_async_copy(src, dst, load_sem.at[n]) for n, (src, dst) in enumerate(zip(inputs, rest[8:]))]
     for load in loads:
         load.start()
     greet(True, True)
@@ -491,6 +515,12 @@
     )
     gbuf[(y * 2 + c) * 4 + x] = chunk.astype(BF16)
     prepare(position, work)
+    damp = damp_ref[0, 0]
+    half, start, _, _, _ = place(position)
+    x_ref, dg_ref = work[0], work[3]
+    x_ref[pl.ds(0, XROWS), :] = chunk[:XROWS]
+    partial_diagonal(x_ref, dg_ref, position, count_ref[0, 0], damp, part_ref, rows_out)
+    rows_in[pl.ds(position, 1), :] = rows_out[pl.ds(position, 1), :]
     greeted(True, True)
 
     def spread_copy(dy, dx):
@@ -514,13 +544,52 @@
     for dy, dx in plane_offsets():
         spread_copy(dy, dx).start()
 
+    def row_copy(d):
+        other, _ = plane_peer(d)
+        return pltpu.make_async_remote_copy(
+            src_ref=rows_out.at[pl.ds(other, 1), :], dst_ref=rows_in.at[pl.ds(position, 1), :],
+            send_sem=row_sem.at[0], recv_sem=row_sem.at[1], device_id=(other, cam), device_id_type=MESH,
+        )
+
+    def send_row(d, carry):
+        row_copy(d).start()
+        return carry
+
+    lax.fori_loop(1, PTS, send_row, 0)
+
+    def all_rows():
+        return pltpu.make_async_remote_copy(
+            src_ref=rows_out.at[pl.ds(0, PTS - 1), :], dst_ref=rows_in.at[pl.ds(0, PTS - 1), :],
+            send_sem=row_sem.at[0], recv_sem=row_sem.at[1], device_id=plane_peer(1), device_id_type=MESH,
+        )
+
+    zd_ref, pd_ref = vectors[:2]
+    zd = Exchange(False, blocks_of(zd_ref, 8), zd_sem)
+    pd = Exchange(True, blocks_of(pd_ref, 8), pd_sem)
+
+    def diagonal_rows():
+        all_rows().wait_recv()
+        own = jnp.sum(rows_in[...], axis=0, keepdims=True)
+        sub = iota((8, 128), 0)
+        mine = (iota((8, 128), 1) - start + 128) % 128 < 72
+        first, second = groups_ref[0, 0].astype(F32), groups_ref[0, 1].astype(F32)
+        value = jnp.where(sub == 0, jnp.where(mine, own, 0.0), jnp.where(sub == 1, first, second))
+        zd_ref[pl.ds(pl.multiple_of(cam * 8, 8), 8), :] = value
+        zd.send()
+
+    def diagonal_groups():
+        zd.receive()
+        pd_ref[pl.ds(pl.multiple_of(position * 8, 8), 8), :] = by_group(zd_ref, half, lambda t: spread(zd_ref, t * 8))
+        pd.send()
+
     def hand_on(row, count):
         chunks((row * 2 + c) * 4, count)(send_sem.at[0], recv_sem.at[row]).wait_recv()
         share(row, c).start()
 
     def assemble(*accs):
-        group, finish = make_group(lambda s: gbuf[s], count_ref[0, 0], damp_ref[0, 0], position, dq_ref, work, accs)
+        group, finish = make_group(lambda s: gbuf[s], count_ref[0, 0], damp, position, work, accs)
         hand_on(y, 3)
+        diagonal_rows()
         hand_on((y + 1) % 4, 4)
 
         def one(step, carry):
@@ -532,6 +601,10 @@
             def _():
                 hand_on((y + step + 2) % 4, 4)
 
+            @pl.when(step == 1)
+            def _():
+                diagonal_groups()
+
             return carry
 
         lax.fori_loop(0, 4, one, 0)
@@ -546,12 +619,14 @@
 
     def settle():
         store.wait()
+        all_rows().wait_send()
+        zd.sent()
         chunks(0, 15)(send_sem.at[0], recv_sem.at[0]).wait_send()
         for row in range(4):
             share(row, c).wait_send()
 
     solve(
-        tile_ref, lambda h: total_diag(dq_ref, h), groups_ref, damp_ref[0, 0], rhs_ref, out_ref, *vectors, sems,
+        tile_ref, groups_ref, damp, rhs_ref, out_ref, *vectors, pd, sems,
         unpack, settle,
     )
 
@@ -578,11 +653,12 @@
         out_shape=(jax.ShapeDtypeStruct((72, 2304), F32), jax.ShapeDtypeStruct((9, 8, 128), F32)),
         in_specs=[far] * 7,
         out_specs=(far, vm),
-        scratch_shapes=[pltpu.VMEM((PTS, ROWS, 128), BF16), pltpu.VMEM((72, 2304), F32), pltpu.VMEM((2, 656, 128), F32), pltpu.VMEM((4, 2, 16, 128), F32)]
+        scratch_shapes=[pltpu.VMEM((PTS, ROWS, 128), BF16), pltpu.VMEM((72, 2304), F32), pltpu.VMEM((2, 656, 128), F32), pltpu.VMEM((2, 16, 128), F32)]
+        + [pltpu.VMEM((PTS, 128), F32), pltpu.VMEM((PTS, 128), F32)]
         + scratch()
         + solve_scratch()
         + solve_sems()
-        + [pltpu.SemaphoreType.DMA((n,)) for n in (1, 4, 4, 4, 8)]
+        + [pltpu.SemaphoreType.DMA((n,)) for n in (1, 4, 4, 4, 8, 2, 2, 2)]
         + [pltpu.SMEM((1, 1), jnp.int32), pltpu.SMEM((1, 1), F32), pltpu.SMEM((1, 2), jnp.int32)]
         + [pltpu.VMEM((72, 128), BF16), pltpu.VMEM((24, 128), BF16), pltpu.VMEM((4, 128), jnp.int32), pltpu.VMEM((9, 8, 128), F32)],
         compiler_params=pltpu.CompilerParams(collective_id=0, has_side_effects=True, vmem_limit_bytes=60 * 2**20),

time: 56.3 us -> 53.7 us (0.954)
  Pallas kernels: 54.2 us -> 51.6 us
    pallas_call x1, Pallas kernels: 52.3 us -> 49.7 us  [body(): pl.pallas_call(whole_kernel, out_shape=(jax.ShapeDtypeStruct((72, 2304),...]
where the time goes in v3:
time: 53.7 us; the launch traced here: 53.5 us
  Pallas kernels  51.6 us (96%)
  between operations  1.93 us (4%)
    pallas_call x1, Pallas kernels, body(): pl.pallas_call(whole_kernel, out_shape=(jax.ShapeDtypeStruct((72, 2304),...  49.7 us
    pallas_call x1, Pallas kernels, body(): pl.pallas_call(hand_over, out_shape=(jax.ShapeDtypeStruct((72, 2304), F32...  1.91 us

profile of v3, /device:TPU:1, one launch (start us, length us, event | category | flops | bytes accessed | tf_op | source)
XLA Modules:
  0.0 53.5 jit_solution(10402530783158985532)
XLA Ops:
  1.9 49.7 %reduced_system.1 = (f32[72,2304]{1,0:T(8,128)}, f32[9,8,128]{2,1,0:T(8,128)}) custom-call(s32[1,1]{1,0:T(1,128)} %bitcast.8.count_in, f32[1,1]{1,0:T(1,128)} %bitcast.9.damp_in, s32[1,2]{1,0:T(1,128)} %groups_in.1, bf16[72,128]{1,0:T(8,128)(2,1)} %bitcast.11, bf16[24,128]{1,0:T(8,128)(2,1)} %bitcast.12, s32[4,128]{1,0:T(4,128)} %bitcast.13, ...), custom_call_target="tpu_custom_call" | custom-call | tf_op jit(solution)/shard_map/reduced_system/pallas_call | solution.py:651
  51.6 1.9 %hand_over.1 = (f32[72,2304]{1,0:T(8,128)}, f32[9,8,128]{2,1,0:T(8,128)}) custom-call(f32[72,2304]{1,0:T(8,128)} %get-tuple-element.6.tile_in, f32[9,8,128]{2,1,0:T(8,128)} %get-tuple-element.7.solved_in), custom_call_target="tpu_custom_call" | custom-call | tf_op jit(solution)/shard_map/hand_over/pallas_call | solution.py:670

commit v4 on v3

--- a/solution.py
+++ b/solution.py
@@ -460,8 +460,12 @@
     return [pltpu.SemaphoreType.DMA((2,)) for _ in range(4)]
 
 
-def plane_offsets():
-    return [(dy, dx) for dy in (0, 3, 2, 1) for dx in range(4) if (dy, dx) != (0, 0)]
+def near_offsets():
+    return [(0, dx, dc) for dc in range(2) for dx in range(4) if (dx, dc) != (0, 0)]
+
+
+def far_offsets():
+    return [(dy, dx, 0) for dy in (3, 2, 1) for dx in range(4)]
 
 
 def partial_diagonal(x_ref, dg_ref, position, count, damp, part_ref, rows_out):
@@ -506,6 +510,7 @@
     for load in loads:
         load.start()
     greet(True, True)
+    prepare(position, work)
     for load in loads:
         load.wait()
     cameras = obs_ref[...]
@@ -514,7 +519,6 @@
         [camera_ref[...].astype(F32), point_ref[...].astype(F32), slot.astype(F32), jnp.zeros((12, 128), F32)], axis=0
     )
     gbuf[(y * 2 + c) * 4 + x] = chunk.astype(BF16)
-    prepare(position, work)
     damp = damp_ref[0, 0]
     half, start, _, _, _ = place(position)
     x_ref, dg_ref = work[0], work[3]
@@ -523,9 +527,9 @@
     rows_in[pl.ds(position, 1), :] = rows_out[pl.ds(position, 1), :]
     greeted(True, True)
 
-    def spread_copy(dy, dx):
+    def spread_copy(dy, dx, dc):
         own = gbuf.at[(y * 2 + c) * 4 + x]
-        other = ((y + dy) % 4 * 4 + (x + dx) % 4) * 2 + c
+        other = ((y + dy) % 4 * 4 + (x + dx) % 4) * 2 + (c + dc) % 2
         return pltpu.make_async_remote_copy(
             src_ref=own, dst_ref=own, send_sem=send_sem.at[0], recv_sem=recv_sem.at[y],
             device_id=(other, cam), device_id_type=MESH,
@@ -541,8 +545,8 @@
     def share(row, core):
         return chunks((row * 2 + core) * 4, 4)(share_send.at[row], share_recv.at[row])
 
-    for dy, dx in plane_offsets():
-        spread_copy(dy, dx).start()
+    for offset in near_offsets():
+        spread_copy(*offset).start()
 
     def row_copy(d):
         other, _ = plane_peer(d)
@@ -556,6 +560,8 @@
         return carry
 
     lax.fori_loop(1, PTS, send_row, 0)
+    for offset in far_offsets():
+        spread_copy(*offset).start()
 
     def all_rows():
         return pltpu.make_async_remote_copy(
@@ -582,27 +588,32 @@
         pd_ref[pl.ds(pl.multiple_of(position * 8, 8), 8), :] = by_group(zd_ref, half, lambda t: spread(zd_ref, t * 8))
         pd.send()
 
-    def hand_on(row, count):
-        chunks((row * 2 + c) * 4, count)(send_sem.at[0], recv_sem.at[row]).wait_recv()
+    def hand_on(row):
+        chunks((row * 2 + c) * 4, 4)(send_sem.at[0], recv_sem.at[row]).wait_recv()
         share(row, c).start()
 
     def assemble(*accs):
         group, finish = make_group(lambda s: gbuf[s], count_ref[0, 0], damp, position, work, accs)
-        hand_on(y, 3)
         diagonal_rows()
-        hand_on((y + 1) % 4, 4)
+        chunks(y * 8, 7)(send_sem.at[0], recv_sem.at[y]).wait_recv()
+        hand_on((y + 1) % 4)
 
         def one(step, carry):
             row = (y + step) % 4
-            share(row, 1 - c).wait_recv()
+
+            @pl.when(step > 0)
+            def _():
+                share(row, 1 - c).wait_recv()
+
             group(row)
 
-            @pl.when(step < 2)
+            @pl.when(step == 0)
             def _():
-                hand_on((y + step + 2) % 4, 4)
+                hand_on((y + 2) % 4)
 
             @pl.when(step == 1)
             def _():
+                hand_on((y + 3) % 4)
                 diagonal_groups()
 
             return carry
@@ -621,9 +632,9 @@
         store.wait()
         all_rows().wait_send()
         zd.sent()
-        chunks(0, 15)(send_sem.at[0], recv_sem.at[0]).wait_send()
-        for row in range(4):
-            share(row, c).wait_send()
+        chunks(0, 19)(send_sem.at[0], recv_sem.at[0]).wait_send()
+        for step in range(1, 4):
+            share((y + step) % 4, c).wait_send()
 
     solve(
         tile_ref, groups_ref, damp, rhs_ref, out_ref, *vectors, pd, sems,

time: 53.7 us -> 52.1 us (0.970)
  Pallas kernels: 51.6 us -> 50 us
    pallas_call x1, Pallas kernels: 49.7 us -> 48.1 us  [body(): pl.pallas_call(whole_kernel, out_shape=(jax.ShapeDtypeStruct((72, 2304),...]
where the time goes in v4:
time: 52.1 us; the launch traced here: 51.9 us
  Pallas kernels  50 us (96%)
  between operations  1.93 us (4%)
    pallas_call x1, Pallas kernels, body(): pl.pallas_call(whole_kernel, out_shape=(jax.ShapeDtypeStruct((72, 2304),...  48.1 us
    pallas_call x1, Pallas kernels, body(): pl.pallas_call(hand_over, out_shape=(jax.ShapeDtypeStruct((72, 2304), F32...  1.91 us

profile of v4, /device:TPU:1, one launch (start us, length us, event | category | flops | bytes accessed | tf_op | source)
XLA Modules:
  0.0 51.9 jit_solution(7879819194389298190)
XLA Ops:
  1.9 48.1 %reduced_system.1 = (f32[72,2304]{1,0:T(8,128)}, f32[9,8,128]{2,1,0:T(8,128)}) custom-call(s32[1,1]{1,0:T(1,128)} %bitcast.8.count_in, f32[1,1]{1,0:T(1,128)} %bitcast.9.damp_in, s32[1,2]{1,0:T(1,128)} %groups_in.1, bf16[72,128]{1,0:T(8,128)(2,1)} %bitcast.11, bf16[24,128]{1,0:T(8,128)(2,1)} %bitcast.12, s32[4,128]{1,0:T(4,128)} %bitcast.13, ...), custom_call_target="tpu_custom_call" | custom-call | tf_op jit(solution)/shard_map/reduced_system/pallas_call | solution.py:662
  50.0 1.9 %hand_over.1 = (f32[72,2304]{1,0:T(8,128)}, f32[9,8,128]{2,1,0:T(8,128)}) custom-call(f32[72,2304]{1,0:T(8,128)} %get-tuple-element.6.tile_in, f32[9,8,128]{2,1,0:T(8,128)} %get-tuple-element.7.solved_in), custom_call_target="tpu_custom_call" | custom-call | tf_op jit(solution)/shard_map/hand_over/pallas_call | solution.py:681

commit v5 on v4

--- a/solution.py
+++ b/solution.py
@@ -253,11 +253,15 @@
 
 
 def unpack_tile(acc_ref, tile_ref):
-    for g in range(9):
+    def one(g, carry):
+        rows = pl.ds(pl.multiple_of(g * 8, 8), 8)
         for h in range(2):
             for j in range(8):
-                tile_ref[pl.ds(g * 8, 8), pl.ds(h * 1152 + j * 128, 128)] = acc_ref[h, pl.ds(g * 64 + j, 8, stride=8), :]
-            tile_ref[pl.ds(g * 8, 8), pl.ds(h * 1152 + 1024, 128)] = acc_ref[h, pl.ds(576 + g * 8, 8), :]
+                tile_ref[rows, pl.ds(h * 1152 + j * 128, 128)] = acc_ref[h, pl.ds(g * 64 + j, 8, stride=8), :]
+            tile_ref[rows, pl.ds(h * 1152 + 1024, 128)] = acc_ref[h, pl.ds(pl.multiple_of(576 + g * 8, 8), 8), :]
+        return carry
+
+    lax.fori_loop(0, 9, one, 0)
 
 
 MESH = pl.DeviceIdType.MESH

time: 52.1 us -> 52.1 us (level)
  no operation moved by 1% of the time
where the time goes in v5:
time: 52.1 us; the launch traced here: 52 us
  Pallas kernels  50 us (96%)
  between operations  1.93 us (4%)
    pallas_call x1, Pallas kernels, body(): pl.pallas_call(whole_kernel, out_shape=(jax.ShapeDtypeStruct((72, 2304),...  48.1 us
    pallas_call x1, Pallas kernels, body(): pl.pallas_call(hand_over, out_shape=(jax.ShapeDtypeStruct((72, 2304), F32...  1.91 us

profile of v5, /device:TPU:1, one launch (start us, length us, event | category | flops | bytes accessed | tf_op | source)
XLA Modules:
  0.0 52.0 jit_solution(9112548163397179125)
XLA Ops:
  1.9 48.1 %reduced_system.1 = (f32[72,2304]{1,0:T(8,128)}, f32[9,8,128]{2,1,0:T(8,128)}) custom-call(s32[1,1]{1,0:T(1,128)} %bitcast.8.count_in, f32[1,1]{1,0:T(1,128)} %bitcast.9.damp_in, s32[1,2]{1,0:T(1,128)} %groups_in.1, bf16[72,128]{1,0:T(8,128)(2,1)} %bitcast.11, bf16[24,128]{1,0:T(8,128)(2,1)} %bitcast.12, s32[4,128]{1,0:T(4,128)} %bitcast.13, ...), custom_call_target="tpu_custom_call" | custom-call | tf_op jit(solution)/shard_map/reduced_system/pallas_call | solution.py:666
  50.0 1.9 %hand_over.1 = (f32[72,2304]{1,0:T(8,128)}, f32[9,8,128]{2,1,0:T(8,128)}) custom-call(f32[72,2304]{1,0:T(8,128)} %get-tuple-element.6.tile_in, f32[9,8,128]{2,1,0:T(8,128)} %get-tuple-element.7.solved_in), custom_call_target="tpu_custom_call" | custom-call | tf_op jit(solution)/shard_map/hand_over/pallas_call | solution.py:685
